TPU v7x, 128 devices: a whole 4x4x4 slice. The times are simulated.
128 devices in a mesh: dp: 16 (over z_hi, y, core), tensor: 8 (over x, z_lo).
Axes of the slice: x: 4, y: 4, z: 4 (z_hi: 2, z_lo: 2; z = z_hi * 2 + z_lo), core: 2. Of those that a mesh axis runs over, the one named last changes fastest.
Arguments:
- hidden_in: bfloat16 [16384, 4096], P(('dp', 'tensor')), may hold values from -500 to 500
- teacher: bfloat16 [16384, 4096], P(('dp', 'tensor')), may hold values from -3 to 3
- row_source: int32 [16384], P(('dp', 'tensor')), may hold values from 0 to 16383, as said below
- segments: int32 [16, 1024], P('dp'), may hold values from 0 to 3, never falling along the last dimension, each value on 1 to 512 neighbouring positions
- branch: bfloat16 [16384, 4096], P(('dp', 'tensor')), may hold values from -3 to 3
- queries: bfloat16 [16384, 4096], P('dp', 'tensor'), may hold values from -6 to 6
- key_rot: bfloat16 [16384, 1024], P('dp', 'tensor'), may hold values from -4 to 4
- value_rows: bfloat16 [16384, 1024], P('dp', 'tensor'), may hold values from -5 to 5
- attended: bfloat16 [16384, 4096], P('dp', 'tensor'), may hold values from -5 to 5
- norm_gain: float32 [4096], replicated, may hold values from 0.1 to 1.9
- w_query: bfloat16 [4096, 4096], P(None, 'tensor'), may hold values from -0.09375 to 0.09375
- w_key: bfloat16 [4096, 1024], P(None, 'tensor'), may hold values from -0.09375 to 0.09375
- w_value: bfloat16 [4096, 1024], P(None, 'tensor'), may hold values from -0.09375 to 0.09375
- w_out: bfloat16 [4096, 4096], P('tensor'), may hold values from -0.09375 to 0.09375
Outputs:
- grad_query: float32 [4096, 4096], P('dp', 'tensor')
- grad_key: float32 [4096, 1024], P('dp', 'tensor')
- grad_value: float32 [4096, 1024], P('dp', 'tensor')
- grad_out: float32 [4096, 4096], P('tensor', 'dp')
- grad_gain: float32 [4096], replicated
- d_hidden_in: float32 [16384, 4096], P(('dp', 'tensor'))
Inputs may be any that keep to these rules, and one draw needn't show every extreme that they name: Student row g takes teacher row row_source[g]; each teacher row is taken once; the teacher row lies on a device of the same tensor index as row g. Of one device's teacher rows at most 9 go to any one device, and in every draw some device sends exactly 9 to some device.
All inputs are finite; a program needn't handle non-finite values.
Results may differ from a plain program's by a relative error of at most 0.018.
Values may be sent and summed in bfloat16 or wider, within the bound.
A program may use at most 192 MiB of HBM per device.

v0:
```python
import jax
import jax.numpy as jnp
from jax import lax
from jax.sharding import PartitionSpec as P

HEADS = 32
KVH = 8
HD = 128


theta_base = 500000.0
eps_norm = 1e-05


def segment_positions(segment_ids):
    row_index = jnp.arange(segment_ids.shape[0], dtype=jnp.int32)
    before = jnp.sum((segment_ids[None, :] < segment_ids[:, None]).astype(jnp.int32), axis=1)
    return row_index - before


def rotation_tables(positions, head_dim):
    half_dim = head_dim // 2
    frequency = theta_base ** (-2.0 * jnp.arange(half_dim, dtype=jnp.float32) / head_dim)
    angles = positions.astype(jnp.float32)[:, None] * frequency[None, :]
    return (jnp.cos(angles), jnp.sin(angles))


def unrotate(values, cos_table, sin_table):
    half_dim = values.shape[-1] // 2
    first_half = values[..., :half_dim]
    second = values[..., half_dim:]
    cosine = cos_table[:, None, :]
    sine_part = sin_table[:, None, :]
    return jnp.concatenate(
        [first_half * cosine + second * sine_part, second * cosine - first_half * sine_part],
        axis=-1,
    )


def relay_teacher(teacher, row_source):
    local_rows = teacher.shape[0]
    dp_count = lax.axis_size("dp")
    tensor_count = lax.axis_size("tensor")
    capacity = local_rows // dp_count + 1
    source_dp = row_source // local_rows // tensor_count
    source_row = row_source % local_rows
    position = jnp.arange(local_rows, dtype=jnp.int32)
    same_source = source_dp[None, :] == source_dp[:, None]
    earlier = position[None, :] < position[:, None]
    slot_rank = jnp.sum((same_source & earlier).astype(jnp.int32), axis=1)
    peer_ids = jnp.arange(dp_count, dtype=jnp.int32)
    slot_ids = jnp.arange(capacity, dtype=jnp.int32)
    wanted = (source_dp[None, None, :] == peer_ids[:, None, None]) & (
        slot_rank[None, None, :] == slot_ids[None, :, None]
    )
    request = jnp.sum(jnp.where(wanted, source_row[None, None, :] + 1, 0), axis=2) - 1
    asked_rows = lax.all_to_all(request, "dp", split_axis=0, concat_axis=0, tiled=True)
    picked = jnp.take(teacher, jnp.maximum(asked_rows, 0).reshape(-1), axis=0).reshape(
        dp_count, capacity, teacher.shape[1]
    )
    parcel = jnp.where((asked_rows >= 0)[:, :, None], picked, jnp.zeros_like(picked))
    arrived = lax.all_to_all(parcel, "dp", split_axis=0, concat_axis=0, tiled=True)
    flat_index = source_dp * capacity + slot_rank
    return jnp.take(arrived.reshape(dp_count * capacity, teacher.shape[1]), flat_index, axis=0)


def per_device(
    hidden_in,
    teacher,
    row_source,
    segments,
    branch,
    queries,
    key_rot,
    value_rows,
    attended,
    norm_gain,
    w_query,
    w_key,
    w_value,
    w_out,
):
    f32 = jnp.float32
    bf16 = jnp.bfloat16
    contract_rows = (((0,), (0,)), ((), ()))
    contract_cols = (((1,), (1,)), ((), ()))
    own_count_rows = hidden_in.shape[0]
    group_rows = lax.all_gather(hidden_in, "tensor", axis=0, tiled=True)
    row_count = group_rows.shape[0]
    query_width = queries.shape[1]
    local_heads = query_width // HD
    local_kv = key_rot.shape[1] // HD
    group_size = HEADS // KVH
    scale = HD ** (-0.5)
    row_total = own_count_rows * lax.axis_size("tensor") * lax.axis_size("dp")
    loss_scale = row_total ** (-0.5)
    own_start = lax.axis_index("tensor") * own_count_rows
    floated = group_rows.astype(f32)
    inv_rms = lax.rsqrt(jnp.mean(floated * floated, axis=1, keepdims=True) + eps_norm)
    unit_rows = floated * inv_rms
    normed = (unit_rows * norm_gain[None, :]).astype(bf16)
    segment_ids = segments[0]
    cos_table, sin_table = rotation_tables(segment_positions(segment_ids), HD)
    grouped = queries.reshape(row_count, local_kv, group_size, HD)
    keys_three = key_rot.reshape(row_count, local_kv, HD)
    values_three = value_rows.reshape(row_count, local_kv, HD)
    row_index = jnp.arange(row_count, dtype=jnp.int32)
    allowed = (segment_ids[:, None] == segment_ids[None, :]) & (
        row_index[None, :] <= row_index[:, None]
    )
    scores = jnp.einsum("qkgd,ckd->kgqc", grouped, keys_three, preferred_element_type=f32) * scale
    scores = jnp.where(allowed, scores, -1e30)
    row_max = jnp.max(scores, axis=-1, keepdims=True)
    weights = jnp.where(allowed, jnp.exp(scores - row_max), 0.0)
    soft_weights = weights / jnp.sum(weights, axis=-1, keepdims=True)
    probs_low = soft_weights.astype(bf16)
    target = relay_teacher(teacher, row_source)
    out_slope = ((branch.astype(f32) - target.astype(f32)) * loss_scale).astype(bf16)
    full_slope = lax.all_gather(out_slope, "tensor", axis=0, tiled=True)
    grad_out = lax.dot_general(attended, full_slope, contract_rows, preferred_element_type=f32)
    d_attended = (
        lax.dot_general(full_slope, w_out, contract_cols, preferred_element_type=f32)
        .astype(bf16)
        .reshape(row_count, local_kv, group_size, HD)
    )
    d_probs = jnp.einsum("qkgd,ckd->kgqc", d_attended, values_three, preferred_element_type=f32)
    row_delta = jnp.sum(soft_weights * d_probs, axis=-1, keepdims=True)
    d_scores = (soft_weights * (d_probs - row_delta) * scale).astype(bf16)
    dv_rows = jnp.einsum("kgqc,qkgd->ckd", probs_low, d_attended, preferred_element_type=f32)
    d_value = dv_rows.astype(bf16).reshape(row_count, local_kv * HD)
    grad_value = lax.dot_general(normed, d_value, contract_rows, preferred_element_type=f32)
    dk_rot = jnp.einsum("kgqc,qkgd->ckd", d_scores, grouped, preferred_element_type=f32)
    d_key = unrotate(dk_rot, cos_table, sin_table).astype(bf16).reshape(row_count, local_kv * HD)
    grad_key = lax.dot_general(normed, d_key, contract_rows, preferred_element_type=f32)
    dq_rot = jnp.einsum("kgqc,ckd->qkgd", d_scores, keys_three, preferred_element_type=f32).reshape(
        row_count, local_heads, HD
    )
    d_query = unrotate(dq_rot, cos_table, sin_table).astype(bf16).reshape(row_count, query_width)
    grad_query = lax.dot_general(normed, d_query, contract_rows, preferred_element_type=f32)
    summed_query, summed_key, summed_value, summed_out = (
        lax.psum_scatter(
            grad_query.astype(jnp.bfloat16), "dp", scatter_dimension=0, tiled=True
        ).astype(jnp.float32),
        lax.psum_scatter(
            grad_key.astype(jnp.bfloat16), "dp", scatter_dimension=0, tiled=True
        ).astype(jnp.float32),
        lax.psum_scatter(
            grad_value.astype(jnp.bfloat16), "dp", scatter_dimension=0, tiled=True
        ).astype(jnp.float32),
        lax.psum_scatter(
            grad_out.astype(jnp.bfloat16), "dp", scatter_dimension=1, tiled=True
        ).astype(jnp.float32),
    )
    own_unit = lax.dynamic_slice_in_dim(unit_rows, own_start, own_count_rows, 0)
    own_inv = lax.dynamic_slice_in_dim(inv_rms, own_start, own_count_rows, 0)
    total = lax.dot_general(d_query, w_query, contract_cols, preferred_element_type=f32)
    total = total + lax.dot_general(d_key, w_key, contract_cols, preferred_element_type=f32)
    d_normed = lax.psum_scatter(
        (
            total + lax.dot_general(d_value, w_value, contract_cols, preferred_element_type=f32)
        ).astype(jnp.bfloat16),
        "tensor",
        scatter_dimension=0,
        tiled=True,
    ).astype(jnp.float32)
    gain_part = jnp.sum(d_normed * own_unit, axis=0)
    grad_gain = lax.psum(gain_part, ("dp", "tensor"))
    scaled = d_normed * norm_gain[None, :]
    d_hidden = own_inv * (scaled - own_unit * jnp.mean(scaled * own_unit, axis=1, keepdims=True))
    return (summed_query, summed_key, summed_value, summed_out, grad_gain, d_hidden)


def solution(mesh):
    return jax.shard_map(
        per_device,
        mesh=mesh,
        in_specs=(
            P(("dp", "tensor"), None),
            P(("dp", "tensor"), None),
            P(("dp", "tensor")),
            P("dp", None),
            P(("dp", "tensor"), None),
            P("dp", "tensor"),
            P("dp", "tensor"),
            P("dp", "tensor"),
            P("dp", "tensor"),
            P(),
            P(None, "tensor"),
            P(None, "tensor"),
            P(None, "tensor"),
            P("tensor", None),
        ),
        out_specs=(
            P("dp", "tensor"),
            P("dp", "tensor"),
            P("dp", "tensor"),
            P("tensor", "dp"),
            P(),
            P(("dp", "tensor"), None),
        ),
        check_vma=False,
    )
```

profile of v0, /device:TPU:0, one launch (start us, length us, event | category | flops | bytes accessed | tf_op | source)
XLA Modules:
  0.0 993.9 jit_solution(10084841218479621109)
XLA Ops:
  9.1 15.3 %all_to_all.11 = s32[16,1,9]{2,1,0:T(1,128)S(1)} all-to-all(s32[16,1,9]{2,1,0:T(1,128)S(1)} %copy.55), channel_id=1, replica_groups=mesh['dp'=16,'tensor'=8] {'dp'}, dimensions={0} | all-to-all | bytes 1152 | tf_op jit(solution)/shard_map/all_to_all | solution.py:57
  37.2 40.9 %all-to-all-done.1 = bf16[16,9,4096]{2,1,0:T(8,128)(2,1)} async-done(((bf16[16,9,4096]{2,1,0:T(8,128)(2,1)}), bf16[16,9,4096]{2,1,0:T(8,128)(2,1)}, u32[]{:S(2)}, u32[]{:S(2)}) %all-to-all-start.1) | async-done | bytes 1179680 | tf_op jit(solution)/shard_map/all_to_all | solution.py:62
  92.1 5.7 copy-done.1
  102.6 100.5 %all-gather.3.cloned.1.call-done = bf16[1024,4096]{1,0:T(8,128)(2,1)} async-done(((bf16[128,4096]{1,0:T(8,128)(2,1)}), bf16[1024,4096]{1,0:T(8,128)(2,1)}) %all-gather.3.cloned.1.call-update) | async-done | bytes 8388624 | tf_op jit(solution)/shard_map/all_gather | solution.py:88
  203.0 5.1 fusion
  208.1 170.4 %all-gather.5.cloned.1.call-done = bf16[1024,4096]{1,0:T(8,128)(2,1)} async-done(((bf16[128,4096]{1,0:T(8,128)(2,1)}), bf16[1024,4096]{1,0:T(8,128)(2,1)}) %all-gather.5.cloned.1.call-update) | async-done | bytes 8388624 | tf_op jit(solution)/shard_map/all_gather | solution.py:119
  378.5 9.2 convolution_convert_fusion.4
  388.8 10.3 %fusion.26 = bf16[1024,128]{0,1:T(8,128)(2,1)} fusion(bf16[1024,4,128]{0,2,1:T(8,128)(2,1)S(1)} %bitcast.141, f32[4,1024]{1,0:T(4,128)S(1)} %copy-done.17, f32[4,1024]{1,0:T(4,128)S(1)} %copy-done.14, f32[1024,1024,4]{1,0,2:T(8,128)} %copy-done.1, pred[1024,1024]{0,1:T(8,128)(4,1)S(1)} %copy-done.4), kind=kOutput, calls=%fused_computation.44 | convolution fusion | flops 1099038720 | bytes 19169280 | tf_op jit(solution)/shard_map/kgqc,qkgd->ckd/dot_general | solution.py:129
  399.1 11.8 %fusion.1 = (f32[4,1024]{1,0:T(4,128)}, f32[1024,4,1024]{0,2,1:T(8,128)}) fusion(f32[4,1024]{1,0:T(4,128)} %fusion.7, f32[4,1024]{1,0:T(4,128)} %copy-done.13, f32[1024,1024,4]{1,0,2:T(8,128)S(1)} %bitcast.132, pred[1024,1024]{0,1:T(8,128)(4,1)} %copy-done.3, bf16[1024,4,128]{0,2,1:T(8,128)(2,1)} %bitcast.142, bf16[1024,128]{1,0:T(8,128)(2,1)} %param.21), kind=kOutput, calls=%fused_computation.8 | convolution fusion | flops 1103097856 | bytes 35962880 | tf_op jit(solution)/shard_map/qkgd,ckd->kgqc/dot_general | solution.py:126
  410.9 9.4 fusion.8
  428.0 7.2 convolution_convert_fusion.3
  435.4 6.0 convolution_bitcast_fusion
  441.8 7.2 convolution_convert_fusion.2
  449.1 11.3 %convolution_convert_fusion.1 = bf16[4096,512]{1,0:T(8,128)(2,1)} fusion(bf16[1024,512]{0,1:T(8,128)(2,1)S(1)} %bitcast.135, f32[4096]{0:T(1024)S(1)} %copy-done.15, f32[1024]{0:T(1024)S(1)} %add_rsqrt_fusion, bf16[1024,4096]{1,0:T(8,128)(2,1)} %all-gather.3.cloned.1.call-done), kind=kOutput, calls=%fused_computation.23 | convolution fusion | flops 4313841664 | bytes 13651968 | tf_op jit(solution)/shard_map/dot_general | solution.py:139
  460.6 10.2 %fusion.13 = bf16[512,4096]{0,1:T(8,128)(2,1)} fusion(bf16[1024,4096]{1,0:T(8,128)(2,1)} %all-gather.5.cloned.1.call-done, bf16[1024,512]{1,0:T(8,128)(2,1)} %param.22), kind=kOutput, calls=%fused_computation.24 | convolution fusion | flops 4297064448 | bytes 13631488 | tf_op jit(solution)/shard_map/dot_general | solution.py:120
  470.9 8.1 fusion.42
  479.0 8.2 fusion.52
  487.2 15.4 %add_convert_fusion = bf16[1024,4096]{1,0:T(8,128)(2,1)} fusion(f32[1024,4096]{1,0:T(8,128)} %fusion.52, f32[1024,4096]{1,0:T(8,128)} %fusion.42, bf16[1024,128]{0,1:T(8,128)(2,1)S(1)} %copy-done.12, bf16[4096,128]{1,0:T(8,128)(2,1)S(1)} %copy-done.11), kind=kOutput, calls=%fused_computation.12 | convolution fusion | flops 1086324736 | bytes 43253760 | tf_op jit(solution)/shard_map/dot_general | solution.py:160
  502.7 11.9 %convert_multiply_fusion = f32[1024,4096]{1,0:T(8,128)} fusion(bf16[1024,4096]{1,0:T(8,128)(2,1)} %all-gather.3.cloned.1.call-done, f32[1024]{0:T(1024)S(1)} %add_rsqrt_fusion), kind=kLoop, calls=%fused_computation.2 | loop fusion | flops 8388608 | bytes 25169920 | tf_op jit(solution)/shard_map/mul | solution.py:100
  516.1 61.5 %reduce-scatter.10.cloned.1.call-done = bf16[256,128]{1,0:T(8,128)(2,1)} async-done(((bf16[4096,128]{1,0:T(8,128)(2,1)}), bf16[256,128]{1,0:T(8,128)(2,1)}) %reduce-scatter.10.cloned.1.call-update) | async-done | bytes 65552 | tf_op jit(solution)/shard_map/reduce_scatter | solution.py:147
  579.2 81.9 %reduce-scatter.6.cloned.1.call-done = bf16[256,512]{1,0:T(8,128)(2,1)} async-done(((bf16[4096,512]{1,0:T(8,128)(2,1)}), bf16[256,512]{1,0:T(8,128)(2,1)}) %reduce-scatter.6.cloned.1.call-update) | async-done | bytes 262160 | tf_op jit(solution)/shard_map/reduce_scatter | solution.py:141
  662.9 81.6 %reduce-scatter.12.cloned.1.call-done = bf16[512,256]{0,1:T(8,128)(2,1)} async-done(((bf16[512,4096]{0,1:T(8,128)(2,1)}), bf16[512,256]{0,1:T(8,128)(2,1)}) %reduce-scatter.12.cloned.1.call-update) | async-done | bytes 262160 | tf_op jit(solution)/shard_map/reduce_scatter | solution.py:150
  746.4 168.2 %reduce-scatter.14.cloned.1.call-done = bf16[128,4096]{1,0:T(8,128)(2,1)} async-done(((bf16[1024,4096]{1,0:T(8,128)(2,1)}), bf16[128,4096]{1,0:T(8,128)(2,1)}) %reduce-scatter.14.cloned.1.call-update) | async-done | bytes 1048592 | tf_op jit(solution)/shard_map/reduce_scatter | solution.py:158
  917.0 66.2 %psum.7 = f32[4096]{0:T(1024)} all-reduce(f32[4096]{0:T(1024)S(1)} %get-tuple-element.37), channel_id=1, replica_groups=mesh['dp'=16,'tensor'=8] {'dp','tensor'}, use_global_device_ids=true, to_apply=%region_13.14 | all-reduce | flops 4096 | bytes 32768 | tf_op jit(solution)/shard_map/psum | solution.py:167
  (104 shorter events, 55.8 us)
Async XLA Ops:
  7.2 463.7 %copy-start = (bf16[4096,128]{1,0:T(8,128)(2,1)S(1)}, bf16[4096,128]{1,0:T(8,128)(2,1)}, u32[]{:S(2)}) copy-start(bf16[4096,128]{1,0:T(8,128)(2,1)} %param.25) | copy-start | bytes 3145732
  7.2 195.8 %all-gather.3.cloned.1.call-start = ((), (), s32[]{:S(2)}) async-start(), calls=%async_computation.7 | async-start | bytes 9437184 | tf_op jit(solution)/shard_map/all_gather | solution.py:88
  32.6 45.4 %all-to-all-start.1 = ((bf16[16,9,4096]{2,1,0:T(8,128)(2,1)}), bf16[16,9,4096]{2,1,0:T(8,128)(2,1)}, u32[]{:S(2)}, u32[]{:S(2)}) async-start(bf16[16,9,4096]{2,1,0:T(8,128)(2,1)} %select_select_fusion), calls=%async_computation.1 | async-start | bytes 4194304 | tf_op jit(solution)/shard_map/all_to_all | solution.py:62
  37.1 341.4 %all-gather.5.cloned.1.call-start = ((), (), s32[]{:S(2)}) async-start(), calls=%async_computation.8 | async-start | bytes 9437184 | tf_op jit(solution)/shard_map/all_gather | solution.py:119
  79.9 8.9 copy-start.9
  83.9 430.8 %reduce-scatter.8.cloned.1.call-start = ((), (), s32[]{:S(2)}) async-start(), calls=%async_computation.10 | async-start | bytes 1114112 | tf_op jit(solution)/shard_map/reduce_scatter | solution.py:144
  85.9 6.2 copy-start.5
  92.1 10.5 %copy-start.13 = (f32[4,1024]{1,0:T(4,128)}, f32[4,1024]{1,0:T(4,128)S(1)}, u32[]{:S(2)}) copy-start(f32[4,1024]{1,0:T(4,128)S(1)} %get-tuple-element.50) | copy-start | bytes 49156
  378.5 10.3 %copy-start.4 = (pred[1024,1024]{0,1:T(8,128)(4,1)S(1)}, pred[1024,1024]{0,1:T(8,128)(4,1)}, u32[]{:S(2)}) copy-start(pred[1024,1024]{0,1:T(8,128)(4,1)} %copy-done.3) | copy-start | bytes 3145732
  378.5 10.3 %copy-start.14 = (f32[4,1024]{1,0:T(4,128)S(1)}, f32[4,1024]{1,0:T(4,128)}, u32[]{:S(2)}) copy-start(f32[4,1024]{1,0:T(4,128)} %copy-done.13) | copy-start | bytes 49156
  378.5 10.3 %copy-start.17 = (f32[4,1024]{1,0:T(4,128)S(1)}, f32[4,1024]{1,0:T(4,128)}, u32[]{:S(2)}) copy-start(f32[4,1024]{1,0:T(4,128)} %fusion.7) | copy-start | bytes 49156
  378.5 20.6 %slice-start = ((s8[16777216]{0:T(1024)(128)(4,1)}), s8[4194304]{0:T(1024)(128)(4,1)S(1)}, s32[]{:S(2)}) async-start(s8[16777216]{0:T(1024)(128)(4,1)} %bitcast.131), calls=%async_computation.14 | async-start | bytes 8388608
  378.5 20.6 %slice-start.1 = ((s8[16777216]{0:T(1024)(128)(4,1)}), s8[4194304]{0:T(1024)(128)(4,1)S(1)}, s32[]{:S(2)}) async-start(s8[16777216]{0:T(1024)(128)(4,1)} %bitcast.131), calls=%async_computation.15 | async-start | bytes 8388608
  388.8 10.3 %slice-start.2 = ((s8[16777216]{0:T(1024)(128)(4,1)}), s8[4194304]{0:T(1024)(128)(4,1)S(1)}, s32[]{:S(2)}) async-start(s8[16777216]{0:T(1024)(128)(4,1)} %bitcast.131), calls=%async_computation.16 | async-start | bytes 8388608
  388.8 10.3 %slice-start.3 = ((s8[16777216]{0:T(1024)(128)(4,1)}), s8[4194304]{0:T(1024)(128)(4,1)S(1)}, s32[]{:S(2)}) async-start(s8[16777216]{0:T(1024)(128)(4,1)} %bitcast.131), calls=%async_computation.17 | async-start | bytes 8388608
  410.9 12.6 %copy-start.6 = (bf16[1024,512]{0,1:T(8,128)(2,1)S(1)}, bf16[1024,512]{0,1:T(8,128)(2,1)}, u32[]{:S(2)}) copy-start(bf16[1024,512]{0,1:T(8,128)(2,1)} %copy-done.5) | copy-start | bytes 3145732
  428.0 7.3 copy-start.10
  435.3 6.5 copy-start.12
  435.3 142.3 %reduce-scatter.10.cloned.1.call-start = ((), (), s32[]{:S(2)}) async-start(), calls=%async_computation.11 | async-start | bytes 1114112 | tf_op jit(solution)/shard_map/reduce_scatter | solution.py:147
  449.0 212.0 %reduce-scatter.6.cloned.1.call-start = ((), (), s32[]{:S(2)}) async-start(), calls=%async_computation.9 | async-start | bytes 4456448 | tf_op jit(solution)/shard_map/reduce_scatter | solution.py:141
  460.4 284.1 %reduce-scatter.12.cloned.1.call-start = ((), (), s32[]{:S(2)}) async-start(), calls=%async_computation.12 | async-start | bytes 4456448 | tf_op jit(solution)/shard_map/reduce_scatter | solution.py:150
  470.8 443.7 %reduce-scatter.14.cloned.1.call-start = ((), (), s32[]{:S(2)}) async-start(), calls=%async_computation.13 | async-start | bytes 9437184 | tf_op jit(solution)/shard_map/reduce_scatter | solution.py:158
  470.9 8.1 copy-start.18
  479.0 8.2 copy-start.11
  (8 other events, 35.9 us)
Sparse Core Ops, SparseCore 0:
  9.7 193.3 all-gather.2
  204.7 173.7 all-gather.4
  435.4 72.1 reduce-scatter.7
  511.8 65.7 reduce-scatter.9
  581.6 79.4 reduce-scatter.5
  665.5 78.9 reduce-scatter.11
  746.9 167.6 reduce-scatter.13
where the time goes:
time: 999 us; the launch traced here: 994 us
  waiting for transfers between devices  706 us (71%)
  matrix products  111 us (11%)
  blocking collectives  81.5 us (8%)
  other arithmetic  52.6 us (5%)
  local copies, waits for them, and re-layouts  23.1 us (2%)
  between operations  14.7 us (1%)
    all_gather x1, waiting for transfers between devices, per_device(): full_slope = lax.all_gather(out_slope, 'tensor', axis=0, tiled=True)  170 us
    reduce_scatter x1, waiting for transfers between devices, per_device(): lax.psum_scatter((total + lax.dot_general(d_value, w_value, contract_cols...  168 us
    all_gather x1, waiting for transfers between devices, per_device(): group_rows = lax.all_gather(hidden_in, 'tensor', axis=0, tiled=True)  100 us
    reduce_scatter x1, waiting for transfers between devices, per_device(): lax.psum_scatter(grad_query.astype(jnp.bfloat16), 'dp', scatter_dimension...  81.9 us
    reduce_scatter x1, waiting for transfers between devices, per_device(): lax.psum_scatter(grad_out.astype(jnp.bfloat16), 'dp', scatter_dimension=1...  81.6 us
    psum x1, blocking collectives, per_device(): grad_gain = lax.psum(gain_part, ('dp', 'tensor'))  66.2 us
    reduce_scatter x1, waiting for transfers between devices, per_device(): lax.psum_scatter(grad_value.astype(jnp.bfloat16), 'dp', scatter_dimension...  61.5 us
    all_to_all x1, waiting for transfers between devices, relay_teacher(): lax.all_to_all(parcel, 'dp', split_axis=0, concat_axis=0, tiled=True)  40.9 us
  transfers between devices with their start and end apart: 8, of which 7 were waited for; matrix products, arithmetic and copies ran while one was open for 12% of the time, Pallas kernels for 0%

commit v1 on v0

v1 whole, which is shorter than its diff:
```python
import functools

import jax
import jax.numpy as jnp
from jax import lax
from jax.experimental import pallas as pl
from jax.experimental.pallas import tpu as pltpu
from jax.sharding import PartitionSpec as P

HEADS = 32
KVH = 8
HD = 128
D = 4096
ROWS = 128
GROUP = 1024
N_DP = 16
N_TENSOR = 8
SLOTS = 16
PIECE = 32

MESH = pl.DeviceIdType.MESH
f32 = jnp.float32
bf16 = jnp.bfloat16
NT = (((1,), (1,)), ((), ()))

theta_base = 500000.0
eps_norm = 1e-05


def segment_positions(segment_ids):
    row_index = jnp.arange(segment_ids.shape[0], dtype=jnp.int32)
    before = jnp.sum((segment_ids[None, :] < segment_ids[:, None]).astype(jnp.int32), axis=1)
    return row_index - before


def place():
    d, t = lax.axis_index("dp"), lax.axis_index("tensor")
    return d, t, lax.div(t, 2), lax.rem(t, 2)


def tensor_index(x, z):
    return x * 2 + z


def greet(ids):
    barrier = pltpu.get_barrier_semaphore()
    for device in ids:
        pl.semaphore_signal(barrier, inc=1, device_id=device, device_id_type=MESH)
    pl.semaphore_wait(barrier, len(ids))


def remote(src, dst, send_sem, recv_sem, to):
    return pltpu.make_async_remote_copy(
        src_ref=src, dst_ref=dst, send_sem=send_sem, recv_sem=recv_sem, device_id=to, device_id_type=MESH
    )


class TreeGather:
    def __init__(self, own, full, send, recv):
        self.own, self.full, self.send_sems, self.recv_sems = own, full, send, recv
        self.d, self.t, self.x, self.z = place()
        self.copies = []
        d, x, z = self.d, self.x, self.z
        right, left, across, other = lax.rem(x + 1, 4), lax.rem(x + 3, 4), lax.rem(x + 2, 4), 1 - z
        self.to_right = (d, tensor_index(right, z))
        self.to_left = (d, tensor_index(left, z))
        self.to_z = (d, tensor_index(x, other))
        self.near = [tensor_index(x, other), tensor_index(left, z), tensor_index(right, z), tensor_index(across, z)]
        self.far = [tensor_index(left, other), tensor_index(right, other), tensor_index(across, other)]

    def piece(self, s, p):
        return self.full.at[pl.ds(pl.multiple_of(s * ROWS + p * PIECE, PIECE), PIECE)]

    def send(self, s, p, to, own=False):
        src = self.own.at[pl.ds(p * PIECE, PIECE)] if own else self.piece(s, p)
        copy = remote(src, self.piece(s, p), self.send_sems.at[len(self.copies)], self.recv_sems.at[s, p], to)
        copy.start()
        self.copies.append(copy)

    def wait(self, s, p):
        piece = self.piece(s, p)
        remote(piece, piece, self.send_sems.at[0], self.recv_sems.at[s, p], self.to_z).wait_recv()

    def begin(self):
        t = self.t
        for p, to in [
            (0, self.to_z), (2, self.to_right), (3, self.to_left), (1, self.to_z), (3, self.to_right), (2, self.to_left),
            (2, self.to_z), (0, self.to_right), (1, self.to_left), (3, self.to_z), (1, self.to_right), (0, self.to_left),
        ]:
            self.send(t, p, to, True)

    def steps(self):
        partner, left, right, across = self.near
        far_left, far_right, far_across = self.far
        to_z, to_left, to_right = self.to_z, self.to_left, self.to_right
        plan = [
            (partner, 0, (to_right, to_left)), (partner, 1, (to_left, to_right)),
            (left, 2, (to_right, to_z)), (right, 3, (to_left, to_z)), (left, 3, (to_z,)), (right, 2, (to_z,)),
            (left, 0, (to_right,)), (right, 1, (to_left,)), (across, 2, (to_z,)), (across, 3, (to_z,)),
            (far_left, 0, (to_right,)), (far_right, 1, (to_left,)),
            (left, 1, ()), (right, 0, ()), (across, 0, ()), (across, 1, ()),
            (far_left, 1, ()), (far_right, 0, ()), (far_across, 0, ()), (far_across, 1, ()),
        ] + [(s, p, ()) for s in (partner, far_left, far_right, far_across) for p in (2, 3)]

        def make(s, p, targets):
            def step():
                self.wait(s, p)
                for to in targets:
                    self.send(s, p, to)
            return step

        return [make(*entry) for entry in plan]

    def finish(self):
        for copy in self.copies:
            copy.wait_send()


def gather_kernel(
    source_ref, teacher_ref, branch_ref, hidden_ref,
    hidden_out, slope_out,
    sources, parcel, arrived, slope,
    source_send, source_recv, parcel_send, parcel_recv, hidden_send, hidden_recv, slope_send, slope_recv, local_sem,
):
    d, t, x, z = place()
    peers = [(lax.rem(d + k, N_DP), t) for k in range(1, N_DP)]
    hidden_tree = TreeGather(hidden_ref, hidden_out, hidden_send, hidden_recv)
    slope_tree = TreeGather(slope, slope_out, slope_send, slope_recv)
    greet(peers + [hidden_tree.to_right, hidden_tree.to_left, hidden_tree.to_z])

    source_copies = []
    for k, to in enumerate(peers):
        copy = remote(source_ref, sources.at[d], source_send.at[k], source_recv.at[k], to)
        copy.start()
        source_copies.append(copy)
    hidden_tree.begin()
    own_rows = pl.ds(pl.multiple_of(t * ROWS, ROWS), ROWS)
    keep_hidden = pltpu.make_async_copy(hidden_ref, hidden_out.at[own_rows], local_sem.at[0])
    keep_hidden.start()
    sources[d] = source_ref[...]

    above = (
        lax.broadcasted_iota(jnp.int32, (ROWS, ROWS), 0) < lax.broadcasted_iota(jnp.int32, (ROWS, ROWS), 1)
    ).astype(bf16)
    slot_ids = lax.broadcasted_iota(jnp.int32, (SLOTS, ROWS), 0)
    peer_ids = lax.broadcasted_iota(jnp.int32, (N_DP, ROWS), 0)
    row_ids = lax.broadcasted_iota(jnp.int32, (ROWS, ROWS), 0)

    def slot_onehot(mask, rank, q):
        return ((slot_ids == rank[q:q + 1]) & (mask[q:q + 1] > 0)).astype(f32).astype(bf16)

    def ranks(mask):
        return jnp.dot(mask.astype(bf16), above, preferred_element_type=f32).astype(jnp.int32)

    own_source = source_ref[0:1, :]
    from_peer = (peer_ids == lax.shift_right_logical(own_source, 10)).astype(f32)
    from_rank = ranks(from_peer)
    place_rows = jnp.concatenate([slot_onehot(from_peer, from_rank, q) for q in range(N_DP)], axis=0)
    place_rows = place_rows.astype(f32).T.astype(bf16)

    for copy in source_copies:
        copy.wait_recv()
    wanted = jnp.concatenate([sources[q, 0:1, :] for q in range(N_DP)], axis=0)
    mine = (lax.shift_right_logical(wanted, 10) == d).astype(f32)
    rank = ranks(mine)
    local_row = jnp.bitwise_and(wanted, ROWS - 1)
    picks = []
    for q in range(N_DP):
        row_onehot = (row_ids == local_row[q:q + 1]).astype(f32).astype(bf16)
        picks.append(lax.dot_general(slot_onehot(mine, rank, q), row_onehot, NT, preferred_element_type=f32))
    pick = jnp.concatenate(picks, axis=0).astype(bf16)
    for n in range(0, D, 512):
        parcel[:, n:n + 512] = jnp.dot(pick, teacher_ref[:, n:n + 512], preferred_element_type=f32).astype(bf16)

    own_slots = pl.ds(pl.multiple_of(d * SLOTS, SLOTS), SLOTS)
    parcel_copies = []
    for k, to in enumerate(peers):
        slots = pl.ds(pl.multiple_of(to[0] * SLOTS, SLOTS), SLOTS)
        copy = remote(parcel.at[slots], arrived.at[own_slots], parcel_send.at[k], parcel_recv.at[k], to)
        copy.start()
        parcel_copies.append(copy)
    arrived[own_slots, :] = parcel[own_slots, :]

    hidden_steps = hidden_tree.steps()
    for step in hidden_steps[:10]:
        step()
    for copy in parcel_copies:
        copy.wait_recv()
    for n in range(0, D, 512):
        target = jnp.dot(place_rows, arrived[:, n:n + 512], preferred_element_type=f32)
        slope[:, n:n + 512] = ((branch_ref[:, n:n + 512].astype(f32) - target) * (N_DP * GROUP) ** -0.5).astype(bf16)
    slope_tree.begin()
    keep_slope = pltpu.make_async_copy(slope, slope_out.at[own_rows], local_sem.at[1])
    keep_slope.start()
    for step in hidden_steps[10:]:
        step()
    for step in slope_tree.steps():
        step()
    hidden_tree.finish()
    slope_tree.finish()
    for copy in source_copies + parcel_copies:
        copy.wait_send()
    keep_hidden.wait()
    keep_slope.wait()


def gather_call(row_source, teacher, branch, hidden_in):
    any_space = pl.BlockSpec(memory_space=pl.ANY)
    vmem = pl.BlockSpec(memory_space=pltpu.VMEM)
    dma = pltpu.SemaphoreType.DMA
    return pl.pallas_call(
        gather_kernel,
        out_shape=(jax.ShapeDtypeStruct((GROUP, D), bf16), jax.ShapeDtypeStruct((GROUP, D), bf16)),
        in_specs=[vmem, vmem, vmem, any_space],
        out_specs=(any_space, any_space),
        scratch_shapes=[
            pltpu.VMEM((N_DP, 8, ROWS), jnp.int32),
            pltpu.VMEM((N_DP * SLOTS, D), bf16),
            pltpu.VMEM((N_DP * SLOTS, D), bf16),
            pltpu.VMEM((ROWS, D), bf16),
            dma((15,)), dma((15,)), dma((15,)), dma((15,)),
            dma((28,)), dma((8, 4)), dma((28,)), dma((8, 4)), dma((2,)),
        ],
        compiler_params=pltpu.CompilerParams(
            collective_id=1, has_side_effects=True, vmem_limit_bytes=48 * 2**20
        ),
        cost_estimate=pl.CostEstimate(flops=10**9, bytes_accessed=24 * 2**20, transcendentals=0),
    )(jnp.broadcast_to(row_source[None, :], (8, ROWS)), teacher, branch, hidden_in)


def attention_kernel(
    q_ref, k_ref, v_ref, da_ref, seg_row_ref, seg_col_ref, cos_ref, sin_ref,
    dqkv_ref, dqkv_t_ref, dk_acc, dv_acc,
):
    blk = 256
    scale = HD ** -0.5
    dk_acc[...] = jnp.zeros_like(dk_acc)
    dv_acc[...] = jnp.zeros_like(dv_acc)
    k_t = k_ref[...].astype(f32).T.astype(bf16)

    def rotate_back(values, columns):
        u, w = values[:64], values[64:]
        c, s = cos_ref[:, columns], sin_ref[:, columns]
        return jnp.concatenate([u * c + w * s, w * c - u * s], axis=0)

    for i in range(GROUP // blk):
        rows = slice(i * blk, (i + 1) * blk)
        seen = (i + 1) * blk
        allowed = (seg_col_ref[:seen, :] == seg_row_ref[:, rows]) & (
            lax.broadcasted_iota(jnp.int32, (seen, blk), 0) <= lax.broadcasted_iota(jnp.int32, (seen, blk), 1) + i * blk
        )
        for h in range(4):
            cols = slice(h * HD, (h + 1) * HD)
            q = q_ref[rows, cols]
            da = da_ref[rows, cols]
            scores = lax.dot_general(k_ref[:seen, :], q, NT, preferred_element_type=f32) * scale
            scores = jnp.where(allowed, scores, -1e30)
            weights = jnp.where(allowed, jnp.exp(scores - jnp.max(scores, axis=0, keepdims=True)), 0.0)
            soft = weights * (1.0 / jnp.sum(weights, axis=0, keepdims=True))
            d_probs = lax.dot_general(v_ref[:seen, :], da, NT, preferred_element_type=f32)
            delta = jnp.sum(soft * d_probs, axis=0, keepdims=True)
            d_scores = (soft * (d_probs - delta) * scale).astype(bf16)
            dv_acc[:seen, :] += jnp.dot(soft.astype(bf16), da, preferred_element_type=f32)
            dk_acc[:seen, :] += jnp.dot(d_scores, q, preferred_element_type=f32)
            dq_t = jnp.dot(k_t[:, :seen], d_scores, preferred_element_type=f32)
            dq_t = rotate_back(dq_t, rows)
            dqkv_t_ref[cols, rows] = dq_t.astype(bf16)
            dqkv_ref[rows, cols] = dq_t.T.astype(bf16)
    dk_t = rotate_back(dk_acc[...].T, slice(0, GROUP))
    dqkv_t_ref[512:640, :] = dk_t.astype(bf16)
    dqkv_ref[:, 512:640] = dk_t.T.astype(bf16)
    dqkv_t_ref[640:768, :] = dv_acc[...].T.astype(bf16)
    dqkv_ref[:, 640:768] = dv_acc[...].astype(bf16)


def attention_call(queries, key_rot, value_rows, d_attended, segment_ids):
    positions = segment_positions(segment_ids)
    frequency = theta_base ** (-2.0 * jnp.arange(HD // 2, dtype=f32) / HD)
    angles = frequency[:, None] * positions.astype(f32)[None, :]
    vmem = pl.BlockSpec(memory_space=pltpu.VMEM)
    return pl.pallas_call(
        attention_kernel,
        out_shape=(jax.ShapeDtypeStruct((GROUP, 768), bf16), jax.ShapeDtypeStruct((768, GROUP), bf16)),
        in_specs=[vmem] * 8,
        out_specs=(vmem, vmem),
        scratch_shapes=[pltpu.VMEM((GROUP, HD), f32), pltpu.VMEM((GROUP, HD), f32)],
        compiler_params=pltpu.CompilerParams(vmem_limit_bytes=48 * 2**20),
        cost_estimate=pl.CostEstimate(flops=6 * 10**9, bytes_accessed=8 * 2**20, transcendentals=4 * 2**20),
    )(
        queries, key_rot, value_rows, d_attended, segment_ids[None, :], segment_ids[:, None],
        jnp.cos(angles), jnp.sin(angles),
    )


class TreeScatter:
    def __init__(self, part, slots, send, recv):
        self.part, self.slots, self.send_sems, self.recv_sems = part, slots, send, recv
        self.d, self.t, self.x, self.z = place()
        d, x, z = self.d, self.x, self.z
        self.to_right = (d, tensor_index(lax.rem(x + 1, 4), z))
        self.to_left = (d, tensor_index(lax.rem(x + 3, 4), z))
        self.to_z = (d, tensor_index(x, 1 - z))
        names = [(kind, e, p) for e in (0, 1) for p in (0, 1) for kind in ("relay", "right", "left")]
        names += [("z", 0, p) for p in (0, 1)]
        names += [("zz", k, p) for k in range(4) for p in (2, 3)]
        names += [(kind, 0, p) for p in (2, 3) for kind in ("relay", "right", "left")]
        self.index = {name: n for n, name in enumerate(names)}
        self.copies = []

    def dest(self, k, e):
        z = self.z if e == 0 else 1 - self.z
        return tensor_index(lax.rem(self.x + k, 4), z)

    def rows(self, p):
        return pl.ds(p * PIECE, PIECE)

    def send(self, k, e, p, to, name):
        n = self.index[name]
        copy = remote(
            self.part.at[self.dest(k, e), self.rows(p)], self.slots.at[n], self.send_sems.at[len(self.copies)],
            self.recv_sems.at[n], to,
        )
        copy.start()
        self.copies.append(copy)

    def wait(self, name):
        n = self.index[name]
        slot = self.slots.at[n]
        remote(slot, slot, self.send_sems.at[0], self.recv_sems.at[n], self.to_z).wait_recv()

    def add(self, k, e, p, names):
        for name in names:
            self.wait(name)
        s = self.dest(k, e)
        for n in range(0, D, 512):
            columns = slice(n, n + 512)
            total = self.part[s, self.rows(p), columns].astype(f32)
            for name in names:
                total = total + self.slots[self.index[name], :, columns].astype(f32)
            self.part[s, self.rows(p), columns] = total.astype(bf16)

    def begin_z(self):
        for k in (2, 1, 3, 0):
            for p in (2, 3):
                self.send(k, 1, p, self.to_z, ("zz", k, p))

    def begin_x(self, e, p):
        if p % 2 == 0:
            self.send(2, e, p, self.to_left, ("relay", e, p))
            self.send(1, e, p, self.to_right, ("left", e, p))
        else:
            self.send(2, e, p, self.to_right, ("relay", e, p))
            self.send(3, e, p, self.to_left, ("right", e, p))

    def relay(self, e, p):
        if p % 2 == 0:
            self.add(3, e, p, [("relay", e, p)])
            self.send(3, e, p, self.to_left, ("right", e, p))
        else:
            self.add(1, e, p, [("relay", e, p)])
            self.send(1, e, p, self.to_right, ("left", e, p))

    def z_done(self, k, p):
        self.add(k, 0, p, [("zz", k, p)])

    def root_other(self, p):
        self.add(0, 1, p, [("right", 1, p), ("left", 1, p)])
        self.send(0, 1, p, self.to_z, ("z", 0, p))

    def root_names(self, p):
        names = [("right", 0, p), ("left", 0, p)]
        return names + [("z", 0, p)] if p < 2 else names

    def finish(self):
        for copy in self.copies:
            copy.wait_send()


class StageScatter:
    def __init__(self, part, core, ring, half, sems):
        self.part, self.core, self.ring, self.half = part, core, ring, half
        self.core_send, self.core_recv, self.ring_send, self.ring_recv, self.half_send, self.half_recv = sems
        d, t, _, _ = place()
        self.c, self.y, self.zh = lax.rem(d, 2), lax.rem(lax.div(d, 2), 4), lax.div(d, 8)
        self.to_core = (d + 1 - 2 * self.c, t)
        self.to_ring = [((self.zh * 4 + lax.rem(self.y + k, 4)) * 2 + self.c, t) for k in (1, 2, 3)]
        self.to_half = (((1 - self.zh) * 4 + self.y) * 2 + self.c, t)
        self.late = []

    def core_copy(self, j):
        return remote(self.part.at[1 - self.c, j], self.core.at[j], self.core_send.at[j], self.core_recv.at[j], self.to_core)

    def fold_core(self, j):
        self.core_copy(j).wait_recv()
        self.part[self.c, j] = (self.part[self.c, j].astype(f32) + self.core[j].astype(f32)).astype(bf16)

    def fold_and_send_ring(self):
        for k in (2, 1, 3):
            y = lax.rem(self.y + k, 4)
            for half in (0, 1):
                zh = 1 - self.zh if half == 0 else self.zh
                j = zh * 4 + y
                self.fold_core(j)
                copy = remote(
                    self.part.at[self.c, j], self.ring.at[k - 1, half], self.ring_send.at[k - 1, half],
                    self.ring_recv.at[k - 1, half], self.to_ring[k - 1],
                )
                copy.start()
                self.late.append(copy)
        for half in (0, 1):
            self.fold_core((1 - self.zh if half == 0 else self.zh) * 4 + self.y)

    def ring_total(self, half):
        for k in range(3):
            remote(
                self.ring.at[k, half], self.ring.at[k, half], self.ring_send.at[k, half], self.ring_recv.at[k, half],
                self.to_core,
            ).wait_recv()
        j = (1 - self.zh if half == 0 else self.zh) * 4 + self.y
        total = self.part[self.c, j].astype(f32)
        for k in range(3):
            total = total + self.ring[k, half].astype(f32)
        return j, total

    def send_half(self):
        j, total = self.ring_total(0)
        self.part[self.c, j] = total.astype(bf16)
        copy = remote(self.part.at[self.c, j], self.half, self.half_send, self.half_recv, self.to_half)
        copy.start()
        self.late.append(copy)

    def result(self):
        _, total = self.ring_total(1)
        self.late[-1].wait_recv()
        return total + self.half[...].astype(f32)

    def finish(self):
        for copy in self.late:
            copy.wait_send()
        for j in range(8):
            self.core_copy(j).wait_send()


def scatter_kernel(
    dqkv_ref, dqkv_t_ref, wq_ref, wk_ref, wv_ref, hidden_ref, inv_ref, gain_ref, out_part_ref,
    dh_ref, gqkv_ref, gout_ref, ggain_ref,
    part, slots, qkv_part, qkv_core, qkv_ring, qkv_half, out_part, out_core, out_ring, out_half,
    gain_sum, gain_block, gain_tensor, gain_dp,
    part_send, part_recv,
    qkv_core_send, qkv_core_recv, qkv_ring_send, qkv_ring_recv, qkv_half_send, qkv_half_recv,
    out_core_send, out_core_recv, out_ring_send, out_ring_recv, out_half_send, out_half_recv,
    gain_t_send, gain_t_recv, gain_d_send, gain_d_recv, local_sem,
):
    d, t, x, z = place()
    tree = TreeScatter(part, slots, part_send, part_recv)
    qkv = StageScatter(
        qkv_part, qkv_core, qkv_ring, qkv_half,
        (qkv_core_send, qkv_core_recv, qkv_ring_send, qkv_ring_recv, qkv_half_send.at[0], qkv_half_recv.at[0]),
    )
    out = StageScatter(
        out_part, out_core, out_ring, out_half,
        (out_core_send, out_core_recv, out_ring_send, out_ring_recv, out_half_send.at[0], out_half_recv.at[0]),
    )
    tensor_peers = [(d, lax.rem(t + k, N_TENSOR)) for k in range(1, N_TENSOR)]
    dp_peers = [(lax.rem(d + k, N_DP), t) for k in range(1, N_DP)]
    load = pltpu.make_async_copy(out_part_ref, out_part, local_sem.at[0])
    load.start()
    greet(tensor_peers + dp_peers)
    load.wait()

    for j in range(8):
        out.core_copy(j).start()

    gain_sum[...] = jnp.zeros_like(gain_sum)

    def partials(first):
        rows = slice(first, first + 64)

        def tile(n, carry):
            columns = pl.ds(pl.multiple_of(n * 256, 256), 256)
            lhs = dqkv_ref[:, rows, :].reshape(512, 768)
            total = lax.dot_general(lhs[:, :512], wq_ref[columns, :], NT, preferred_element_type=f32)
            total += lax.dot_general(lhs[:, 512:640], wk_ref[columns, :], NT, preferred_element_type=f32)
            total += lax.dot_general(lhs[:, 640:768], wv_ref[columns, :], NT, preferred_element_type=f32)
            part[:, rows, columns] = total.astype(bf16).reshape(8, 64, 256)
            unit = hidden_ref[:, rows, columns].astype(f32) * inv_ref[:, rows, :]
            gain_sum[:, columns] += jnp.sum((total * unit.reshape(512, 256)).reshape(64, 8, 256), axis=0)
            return carry

        lax.fori_loop(0, D // 256, tile, 0)

    partials(64)
    tree.begin_z()
    partials(0)
    for e in (1, 0):
        for p in (0, 1):
            tree.begin_x(e, p)

    gain_row = jnp.sum(gain_sum[...], axis=0, keepdims=True)
    for i in range(32):
        gain_block[0, i:i + 1, :] = gain_row[:, i * 128:(i + 1) * 128]
    gain_tensor[t] = gain_block[0]
    gain_copies = []
    for k, to in enumerate(tensor_peers):
        copy = remote(gain_block.at[0], gain_tensor.at[t], gain_t_send.at[k], gain_t_recv.at[k], to)
        copy.start()
        gain_copies.append(copy)

    def projection(core):
        def tile(j, carry):
            columns = pl.ds(pl.multiple_of((2 * j + core) * 256, 256), 256)
            normed = (
                (hidden_ref[:, :, columns].astype(f32) * inv_ref[...]) * gain_ref[:, columns].reshape(1, 1, 256)
            ).astype(bf16).reshape(GROUP, 256)
            qkv_part[core, j] = jnp.dot(dqkv_t_ref[...], normed, preferred_element_type=f32).astype(bf16)
            return carry

        lax.fori_loop(0, 8, tile, 0)

    projection(1 - qkv.c)
    for j in range(8):
        qkv.core_copy(j).start()
    out.fold_and_send_ring()
    projection(qkv.c)
    for e in (1, 0):
        for p in (0, 1):
            tree.relay(e, p)
    qkv.fold_and_send_ring()

    for copy in gain_copies:
        copy.wait_recv()
    gain_total = gain_tensor[0]
    for k in range(1, N_TENSOR):
        gain_total = gain_total + gain_tensor[k]
    gain_block[1] = gain_total
    gain_dp[d] = gain_total
    dp_copies = []
    for k, to in enumerate(dp_peers):
        copy = remote(gain_block.at[1], gain_dp.at[d], gain_d_send.at[k], gain_d_recv.at[k], to)
        copy.start()
        dp_copies.append(copy)

    for p in (2, 3):
        tree.z_done(2, p)
        tree.z_done(1 if p == 2 else 3, p)
        tree.begin_x(0, p)
    for p in (0, 1):
        tree.root_other(p)
    for p in (2, 3):
        tree.z_done(3 if p == 2 else 1, p)
        tree.relay(0, p)
        tree.z_done(0, p)
    out.send_half()
    qkv.send_half()
    gout_ref[...] = out.result()

    for copy in dp_copies:
        copy.wait_recv()
    gain_total = gain_dp[0]
    for k in range(1, N_DP):
        gain_total = gain_total + gain_dp[k]
    ggain_ref[...] = gain_total

    for p in (0, 1, 2, 3):
        names = tree.root_names(p)
        for name in names:
            tree.wait(name)
        rows = slice(p * PIECE, (p + 1) * PIECE)
        total = part[t, rows, :].astype(f32)
        for name in names:
            total = total + slots[tree.index[name]].astype(f32)
        inv = inv_ref[t, rows, :]
        unit = hidden_ref[t, rows, :].astype(f32) * inv
        scaled = total * gain_ref[...]
        mean = jnp.sum(scaled * unit, axis=1, keepdims=True) * (1.0 / D)
        dh_ref[rows, :] = inv * (scaled - unit * mean)
    gqkv_ref[...] = qkv.result()

    tree.finish()
    out.finish()
    qkv.finish()
    for copy in gain_copies + dp_copies:
        copy.wait_send()


def scatter_call(dqkv, dqkv_t, w_query, w_key, w_value, hidden, inv_rms, gain, out_part):
    any_space = pl.BlockSpec(memory_space=pl.ANY)
    vmem = pl.BlockSpec(memory_space=pltpu.VMEM)
    dma = pltpu.SemaphoreType.DMA
    stage_sems = [dma((8,)), dma((8,)), dma((3, 2)), dma((3, 2)), dma((1,)), dma((1,))]
    return pl.pallas_call(
        scatter_kernel,
        out_shape=(
            jax.ShapeDtypeStruct((ROWS, D), f32), jax.ShapeDtypeStruct((768, 256), f32),
            jax.ShapeDtypeStruct((512, 256), f32), jax.ShapeDtypeStruct((32, 128), f32),
        ),
        in_specs=[vmem] * 8 + [any_space],
        out_specs=(vmem,) * 4,
        scratch_shapes=[
            pltpu.VMEM((8, ROWS, D), bf16), pltpu.VMEM((28, PIECE, D), bf16),
            pltpu.VMEM((2, 8, 768, 256), bf16), pltpu.VMEM((8, 768, 256), bf16),
            pltpu.VMEM((3, 2, 768, 256), bf16), pltpu.VMEM((768, 256), bf16),
            pltpu.VMEM((2, 8, 512, 256), bf16), pltpu.VMEM((8, 512, 256), bf16),
            pltpu.VMEM((3, 2, 512, 256), bf16), pltpu.VMEM((512, 256), bf16),
            pltpu.VMEM((8, D), f32), pltpu.VMEM((2, 32, 128), f32),
            pltpu.VMEM((N_TENSOR, 32, 128), f32), pltpu.VMEM((N_DP, 32, 128), f32),
            dma((28,)), dma((28,)),
        ] + stage_sems + stage_sems + [dma((7,)), dma((7,)), dma((15,)), dma((15,)), dma((1,))],
        compiler_params=pltpu.CompilerParams(
            collective_id=2, has_side_effects=True, vmem_limit_bytes=62 * 2**20
        ),
        cost_estimate=pl.CostEstimate(flops=14 * 10**9, bytes_accessed=40 * 2**20, transcendentals=0),
    )(
        dqkv.reshape(8, ROWS, 768), dqkv_t, w_query, w_key, w_value, hidden.reshape(8, ROWS, D),
        inv_rms.reshape(8, ROWS, 1), gain, out_part,
    )


def per_device(
    hidden_in, teacher, row_source, segments, branch, queries, key_rot, value_rows, attended, norm_gain,
    w_query, w_key, w_value, w_out,
):
    hidden, slope = gather_call(row_source, teacher, branch, hidden_in)
    floated = hidden.astype(f32)
    inv_rms = lax.rsqrt(jnp.mean(floated * floated, axis=1, keepdims=True) + eps_norm)
    grad_out = lax.dot_general(attended, slope, (((0,), (0,)), ((), ())), preferred_element_type=f32)
    out_part = jnp.transpose(grad_out.astype(bf16).reshape(512, 8, 2, 256), (2, 1, 0, 3))
    d_attended = lax.dot_general(slope, w_out, NT, preferred_element_type=f32).astype(bf16)
    dqkv, dqkv_t = attention_call(queries, key_rot, value_rows, d_attended, segments[0])
    d_hidden, grad_qkv, grad_out, grad_gain = scatter_call(
        dqkv, dqkv_t, w_query, w_key, w_value, hidden, inv_rms, norm_gain[None, :], out_part
    )
    grads = grad_qkv.T
    return (grads[:, :512], grads[:, 512:640], grads[:, 640:768], grad_out, grad_gain.reshape(D), d_hidden)


def solution(mesh):
    return jax.shard_map(
        per_device,
        mesh=mesh,
        in_specs=(
            P(("dp", "tensor"), None),
            P(("dp", "tensor"), None),
            P(("dp", "tensor")),
            P("dp", None),
            P(("dp", "tensor"), None),
            P("dp", "tensor"),
            P("dp", "tensor"),
            P("dp", "tensor"),
            P("dp", "tensor"),
            P(),
            P(None, "tensor"),
            P(None, "tensor"),
            P(None, "tensor"),
            P("tensor", None),
        ),
        out_specs=(
            P("dp", "tensor"),
            P("dp", "tensor"),
            P("dp", "tensor"),
            P("tensor", "dp"),
            P(),
            P(("dp", "tensor"), None),
        ),
        check_vma=False,
    )
```

time: 999 us -> 318 us (0.32)
  waiting for transfers between devices: 706 us -> 0 us
  Pallas kernels: 0 us -> 262 us
  matrix products: 111 us -> 19.8 us
  blocking collectives: 81.5 us -> 0 us
  other arithmetic: 52.6 us -> 7.39 us
  between operations: 14.7 us -> 0.74 us
    reduce_scatter x5 -> x0, waiting for transfers between devices: 393 us -> none  [the longest x1 168 us: per_device(): lax.psum_scatter((total + lax.dot_general(d_value, w_value, contract_cols...]
    all_gather x2 -> x0, waiting for transfers between devices: 271 us -> none  [the longest x1 170 us: per_device(): full_slope = lax.all_gather(out_slope, 'tensor', axis=0, tiled=True)]
    pallas_call x0 -> x3, Pallas kernels: none -> 262 us  [the longest x1 146 us: gather_call(): pl.pallas_call(gather_kernel, out_shape=(jax.ShapeDtypeStruct((GROUP, D),...]
    dot_general x13 -> x2, matrix products: 111 us -> 19.8 us  [the longest x1 10.1 us: per_device(): lax.dot_general(slope, w_out, NT, preferred_element_type=f32).astype(bf16)]
    psum x1 -> x0, blocking collectives: 66.2 us -> none  [per_device(): grad_gain = lax.psum(gain_part, ('dp', 'tensor'))]
    all_to_all x1 -> x0, waiting for transfers between devices: 40.9 us -> none  [relay_teacher(): lax.all_to_all(parcel, 'dp', split_axis=0, concat_axis=0, tiled=True)]
    mul x2 -> x0, other arithmetic: 15.6 us -> none  [the longest x1 11.9 us: per_device(): unit_rows = floated * inv_rms]
    all_to_all x1 -> x0, blocking collectives: 15.3 us -> none  [relay_teacher(): lax.all_to_all(request, 'dp', split_axis=0, concat_axis=0, tiled=True)]
  transfers between devices with their start and end apart: 8 -> 0, of which waited for: 7 -> 0; matrix products, arithmetic and copies ran while one was open for 12% -> 0% of each run, Pallas kernels for 0% -> 0%
where the time goes in v1:
time: 318 us; the launch traced here: 317 us
  Pallas kernels  262 us (82%)
  local copies, waits for them, and re-layouts  26.7 us (8%)
  matrix products  19.8 us (6%)
  other arithmetic  7.39 us (2%)
    pallas_call x1, Pallas kernels, gather_call(): pl.pallas_call(gather_kernel, out_shape=(jax.ShapeDtypeStruct((GROUP, D),...  146 us
    pallas_call x1, Pallas kernels, scatter_call(): pl.pallas_call(scatter_kernel, out_shape=(jax.ShapeDtypeStruct((ROWS, D),...  102 us
    unnamed x30, local copies, waits for them, and re-layouts  14.7 us
    pallas_call x1, Pallas kernels, attention_call(): pl.pallas_call(attention_kernel, out_shape=(jax.ShapeDtypeStruct((GROUP,...  14.3 us
    dot_general x1, matrix products, per_device(): lax.dot_general(slope, w_out, NT, preferred_element_type=f32).astype(bf16)  10.1 us
    dot_general x1, matrix products, per_device(): lax.dot_general(attended, slope, (((0,), (0,)), ((), ())), preferred_elem...  9.73 us

profile of v1, /device:TPU:0, one launch (start us, length us, event | category | flops | bytes accessed | tf_op | source)
XLA Modules:
  0.0 316.9 jit_solution(1423862398539735778)
XLA Ops:
  1.4 1.3 convert_reduce_fusion
  2.7 1.0 multiply_sine_fusion
  3.7 0.9 copy.29.seg_col_ref
  4.6 1.2 copy-done.2
  5.9 1.2 copy-done.3
  7.1 1.2 copy-done.4
  8.3 146.0 %shard_map.181 = (bf16[1024,4096]{1,0:T(8,128)(2,1)}, bf16[1024,4096]{1,0:T(8,128)(2,1)}) custom-call(s32[8,128]{1,0:T(8,128)S(1)} %broadcast_in_dim.4.source_ref, bf16[128,4096]{1,0:T(8,128)(2,1)S(1)} %copy-done.2, bf16[128,4096]{1,0:T(8,128)(2,1)S(1)} %copy-done.3, bf16[128,4096]{1,0:T(8,128)(2,1)S(1)} %copy-done.4), custom_call_target="tpu_custom_call" | custom-call | flops 1000000000 | bytes 25165824 | tf_op jit(solution)/shard_map/pallas_call | solution.py:211
  154.4 5.1 %multiply_reduce_fusion = f32[1024]{0:T(1024)S(1)} fusion(bf16[1024,4096]{1,0:T(8,128)(2,1)} %get-tuple-element.17), kind=kLoop, calls=%fused_computation | loop fusion | flops 12581888 | bytes 8392704 | tf_op jit(solution)/shard_map/reduce_sum | solution.py:625
  159.5 1.0 copy.31.inv_ref
  160.5 10.1 %convolution_convert_fusion.1.da_ref = bf16[1024,512]{1,0:T(8,128)(2,1)} fusion(bf16[1024,4096]{1,0:T(8,128)(2,1)} %get-tuple-element.14, bf16[512,4096]{1,0:T(8,128)(2,1)} %param.27), kind=kOutput, calls=%fused_computation.3 | convolution fusion | flops 4295491584 | bytes 13631488 | tf_op jit(solution)/shard_map/dot_general | solution.py:628
  170.6 9.7 %convolution_convert_fusion = bf16[4096,512]{1,0:T(8,128)(2,1)} fusion(bf16[1024,4096]{1,0:T(8,128)(2,1)} %get-tuple-element.14, bf16[1024,512]{1,0:T(8,128)(2,1)S(1)} %copy-done), kind=kOutput, calls=%fused_computation.1 | convolution fusion | flops 4297064448 | bytes 13631488 | tf_op jit(solution)/shard_map/dot_general | solution.py:626
  180.3 6.3 %copy.30 = bf16[512,8,2,256]{3,0,1,2:T(8,128)(2,1)} copy(bf16[512,8,2,256]{0,3,2,1:T(8,128)(2,1)} %bitcast.22) | data formatting | bytes 8388608 | tf_op jit(solution)/shard_map/reshape | solution.py:627
  186.7 1.2 copy-done.5
  187.9 1.2 copy-done.9
  189.1 14.3 %shard_map.182 = (bf16[1024,768]{1,0:T(8,128)(2,1)S(1)}, bf16[768,1024]{1,0:T(8,128)(2,1)}) custom-call(bf16[1024,512]{1,0:T(8,128)(2,1)S(1)} %copy-done.5, bf16[1024,128]{1,0:T(8,128)(2,1)S(1)} %copy-done.6, bf16[1024,128]{1,0:T(8,128)(2,1)S(1)} %copy-done.7, bf16[1024,512]{1,0:T(8,128)(2,1)S(1)} %copy-done.9, s32[1,1024]{1,0:T(1,128)S(1)} %copy-done.1, ...), custom_call_target="tpu_custom_call" | custom-call | flops 6000000000 | bytes 8388608 | tf_op jit(solution)/shard_map/pallas_call | solution.py:281
  203.4 1.2 copy-done.8
  204.5 102.0 %shard_map.183 = (f32[128,4096]{1,0:T(8,128)}, f32[768,256]{1,0:T(8,128)}, f32[512,256]{1,0:T(8,128)}, f32[32,128]{1,0:T(8,128)}) custom-call(bf16[8,128,768]{2,1,0:T(8,128)(2,1)} %bitcast.19, bf16[768,1024]{1,0:T(8,128)(2,1)} %get-tuple-element.16.dqkv_t_ref, bf16[4096,512]{1,0:T(8,128)(2,1)} %wq_ref.1, bf16[4096,128]{1,0:T(8,128)(2,1)} %wk_ref.1, ...), custom_call_target="tpu_custom_call" | custom-call | flops 14000000000 | bytes 41943040 | tf_op jit(solution)/shard_map/pallas_call | solution.py:591
  306.6 1.1 fusion
  307.7 1.9 slice.12
  309.6 2.0 copy.32
  311.6 0.8 copy.34
  312.4 0.8 copy.33
  313.1 1.9 copy.38
  315.6 1.3 copy.40
  (23 shorter events, 1.4 us)
Async XLA Ops:
  0.6 169.9 %copy-start = (bf16[1024,512]{1,0:T(8,128)(2,1)S(1)}, bf16[1024,512]{1,0:T(8,128)(2,1)}, u32[]{:S(2)}) copy-start(bf16[1024,512]{1,0:T(8,128)(2,1)} %param.22) | copy-start | bytes 3145732
  4.6 1.2 copy-start.2
  5.9 1.2 copy-start.3
  7.1 1.2 copy-start.4
  180.3 6.4 %copy-start.1 = (s32[1,1024]{1,0:T(1,128)S(1)}, s32[1,1024]{1,0:T(1,128)}, u32[]{:S(2)}) copy-start(s32[1,1024]{1,0:T(1,128)} %seg_row_ref.1) | copy-start | bytes 12292
  180.3 6.4 %copy-start.6 = (bf16[1024,128]{1,0:T(8,128)(2,1)S(1)}, bf16[1024,128]{1,0:T(8,128)(2,1)}, u32[]{:S(2)}) copy-start(bf16[1024,128]{1,0:T(8,128)(2,1)} %k_ref.1) | copy-start | bytes 786436
  180.3 6.4 %copy-start.7 = (bf16[1024,128]{1,0:T(8,128)(2,1)S(1)}, bf16[1024,128]{1,0:T(8,128)(2,1)}, u32[]{:S(2)}) copy-start(bf16[1024,128]{1,0:T(8,128)(2,1)} %v_ref.1) | copy-start | bytes 786436
  186.6 1.2 copy-start.5
  187.9 1.2 copy-start.9
  203.4 1.2 copy-start.8
  306.6 8.4 %copy-start.11 = (f32[32,128]{1,0:T(8,128)S(1)}, f32[32,128]{1,0:T(8,128)}, u32[]{:S(2)}) copy-start(f32[32,128]{1,0:T(8,128)} %get-tuple-element.20) | copy-start | bytes 49156
  306.6 9.0 %copy-start.10 = (f32[128,4096]{1,0:T(8,128)S(1)}, f32[128,4096]{1,0:T(8,128)}, u32[]{:S(2)}) copy-start(f32[128,4096]{1,0:T(8,128)} %get-tuple-element.55) | copy-start | bytes 6291460

commit v2 on v0

v2 whole, which is shorter than its diff:
```python
import jax
import jax.numpy as jnp
import numpy as np
from jax import lax
from jax.experimental import pallas as pl
from jax.experimental.pallas import tpu as pltpu
from jax.sharding import PartitionSpec as P

HEADS = 32
KVH = 8
HD = 128
D = 4096
ROWS = 128
GROUP = 1024
N_DP = 16
N_TENSOR = 8
SLOTS = 16
PIECE = 32
STRIPE = 1024
TILE = 256

MESH = pl.DeviceIdType.MESH
f32 = jnp.float32
bf16 = jnp.bfloat16
NT = (((1,), (1,)), ((), ()))

theta_base = 500000.0
eps_norm = 1e-05


def place():
    d, t = lax.axis_index("dp"), lax.axis_index("tensor")
    return d, t, lax.div(t, 2), lax.rem(t, 2)


def tensor_index(x, z):
    return x * 2 + z


def greet(ids):
    barrier = pltpu.get_barrier_semaphore()
    for device in ids:
        pl.semaphore_signal(barrier, inc=1, device_id=device, device_id_type=MESH)
    pl.semaphore_wait(barrier, len(ids))


def remote(src, dst, send_sem, recv_sem, to):
    return pltpu.make_async_remote_copy(
        src_ref=src, dst_ref=dst, send_sem=send_sem, recv_sem=recv_sem, device_id=to, device_id_type=MESH
    )


class TreeGather:
    def __init__(self, own, full, send, recv, over_z):
        self.over_z = over_z
        self.own, self.full, self.send_sems, self.recv_sems = own, full, send, recv
        self.d, self.t, self.x, self.z = place()
        self.copies = []
        d, x, z = self.d, self.x, self.z
        right, left, across, other = lax.rem(x + 1, 4), lax.rem(x + 3, 4), lax.rem(x + 2, 4), 1 - z
        self.to_right = (d, tensor_index(right, z))
        self.to_left = (d, tensor_index(left, z))
        self.to_z = (d, tensor_index(x, other))
        self.near = [tensor_index(x, other), tensor_index(left, z), tensor_index(right, z), tensor_index(across, z)]
        self.far = [tensor_index(left, other), tensor_index(right, other), tensor_index(across, other)]

    def piece(self, s, p):
        return self.full.at[s, pl.ds(p * PIECE, PIECE)]

    def send(self, s, p, to, own=False):
        src = self.own.at[pl.ds(p * PIECE, PIECE)] if own else self.piece(s, p)
        copy = remote(src, self.piece(s, p), self.send_sems.at[len(self.copies)], self.recv_sems.at[s, p], to)
        copy.start()
        self.copies.append(copy)

    def wait(self, s, p):
        piece = self.piece(s, p)
        remote(piece, piece, self.send_sems.at[0], self.recv_sems.at[s, p], self.to_z).wait_recv()

    def begin(self):
        by_z = list(range(4))
        by_x = list(range(self.over_z, 4)) + list(range(self.over_z))
        for i in (0, 2):
            a, b = by_x[i:i + 2]
            for p, to in (
                (by_z[i], self.to_z), (a, self.to_right), (b, self.to_left), (by_z[i + 1], self.to_z),
                (b, self.to_right), (a, self.to_left),
            ):
                if to is not self.to_z or p < self.over_z or self.over_z < 4:
                    self.send(self.t, p, to, self.own is not None)

    def steps(self):
        partner, left, right, across = self.near
        far_left, far_right, far_across = self.far
        first = list(range(self.over_z))
        last = list(range(self.over_z, 4))
        order = [(partner, p) for p in first[:2]] + [(s, p) for p in (last + first)[:2] for s in (left, right)]
        order += [(partner, p) for p in first[2:]] + [(s, p) for p in (last + first)[2:] for s in (left, right)]
        order += [(s, p) for p in first for s in (far_left, far_right)] + [(across, p) for p in last + first]
        order += [(far_across, p) for p in first]
        order += [(s, p) for s in (partner, far_left, far_right, far_across) for p in last]

        def targets_of(s, p):
            targets = []
            if s is partner and p < self.over_z:
                targets += [self.to_right, self.to_left]
            if s is left and p % 2 == 0 or s is far_left and p % 2 == 0 and p < self.over_z:
                targets.append(self.to_right)
            if s is right and p % 2 == 1 or s is far_right and p % 2 == 1 and p < self.over_z:
                targets.append(self.to_left)
            if p >= self.over_z and (s is left or s is right or s is across):
                targets.append(self.to_z)
            return targets

        plan = [(s, p, targets_of(s, p)) for s, p in order]

        def make(s, p, targets):
            def step():
                self.wait(s, p)
                for to in targets:
                    self.send(s, p, to)
            return step

        return [make(*entry) for entry in plan]

    def finish(self):
        for copy in self.copies:
            copy.wait_send()


class TreeScatter:
    def __init__(self, part, slots, send, recv, over_z):
        self.over_z = over_z
        first, last = range(over_z), range(over_z, 4)
        self.part, self.slots, self.send_sems, self.recv_sems = part, slots, send, recv
        self.d, self.t, self.x, self.z = place()
        d, x, z = self.d, self.x, self.z
        self.to_right = (d, tensor_index(lax.rem(x + 1, 4), z))
        self.to_left = (d, tensor_index(lax.rem(x + 3, 4), z))
        self.to_z = (d, tensor_index(x, 1 - z))
        names = [(kind, e, p) for e in (0, 1) for p in first for kind in ("relay", "right", "left")]
        names += [("z", 0, p) for p in first]
        names += [("zz", k, p) for k in range(4) for p in last]
        names += [(kind, 0, p) for p in last for kind in ("relay", "right", "left")]
        self.index = {name: n for n, name in enumerate(names)}
        self.copies = []

    def dest(self, k, e):
        z = self.z if e == 0 else 1 - self.z
        return tensor_index(lax.rem(self.x + k, 4), z)

    def stripe(self, p):
        return pl.ds(p * STRIPE, STRIPE)

    def send(self, k, e, p, to, name):
        n = self.index[name]
        copy = remote(
            self.part.at[self.dest(k, e), :, self.stripe(p)], self.slots.at[n], self.send_sems.at[len(self.copies)],
            self.recv_sems.at[n], to,
        )
        copy.start()
        self.copies.append(copy)

    def wait(self, name):
        n = self.index[name]
        slot = self.slots.at[n]
        remote(slot, slot, self.send_sems.at[0], self.recv_sems.at[n], self.to_z).wait_recv()

    def total(self, k, e, p, names):
        for name in names:
            self.wait(name)
        total = self.part[self.dest(k, e), :, self.stripe(p)].astype(f32)
        for name in names:
            total = total + self.slots[self.index[name]].astype(f32)
        return total

    def add(self, k, e, p, names):
        self.part[self.dest(k, e), :, self.stripe(p)] = self.total(k, e, p, names).astype(bf16)

    def begin_z(self, p):
        for k in (2, 1, 3, 0):
            self.send(k, 1, p, self.to_z, ("zz", k, p))

    def begin_x(self, e, p):
        if p % 2 == 0:
            self.send(2, e, p, self.to_left, ("relay", e, p))
            self.send(1, e, p, self.to_right, ("left", e, p))
        else:
            self.send(2, e, p, self.to_right, ("relay", e, p))
            self.send(3, e, p, self.to_left, ("right", e, p))

    def relay(self, e, p):
        if p % 2 == 0:
            self.add(3, e, p, [("relay", e, p)])
            self.send(3, e, p, self.to_left, ("right", e, p))
        else:
            self.add(1, e, p, [("relay", e, p)])
            self.send(1, e, p, self.to_right, ("left", e, p))

    def z_done(self, k, p):
        self.add(k, 0, p, [("zz", k, p)])

    def root_other(self, p):
        self.add(0, 1, p, [("right", 1, p), ("left", 1, p)])
        self.send(0, 1, p, self.to_z, ("z", 0, p))

    def result(self, p):
        names = [("right", 0, p), ("left", 0, p)]
        return self.total(0, 0, p, names + [("z", 0, p)] if p < self.over_z else names)

    def finish(self):
        for copy in self.copies:
            copy.wait_send()


class StageScatter:
    def __init__(self, part, core, ring, half, sems):
        self.part, self.core, self.ring, self.half = part, core, ring, half
        self.core_send, self.core_recv, self.ring_send, self.ring_recv, self.half_send, self.half_recv = sems
        d, t, _, _ = place()
        self.c, self.y, self.zh = lax.rem(d, 2), lax.rem(lax.div(d, 2), 4), lax.div(d, 8)
        self.to_core = (d + 1 - 2 * self.c, t)
        self.to_right = ((self.zh * 4 + lax.rem(self.y + 1, 4)) * 2 + self.c, t)
        self.to_left = ((self.zh * 4 + lax.rem(self.y + 3, 4)) * 2 + self.c, t)
        self.to_half = (((1 - self.zh) * 4 + self.y) * 2 + self.c, t)
        self.cut = core.shape[1] // 2
        self.copies = []

    def core_copy(self, j):
        return remote(
            self.part.at[2 * j + 1 - self.c], self.core.at[j], self.core_send.at[j], self.core_recv.at[j], self.to_core
        )

    def block(self, k, half):
        zh = 1 - self.zh if half == 0 else self.zh
        return 2 * (zh * 4 + lax.rem(self.y + k, 4)) + self.c

    def fold_core(self, k, half):
        n = self.block(k, half)
        j = lax.div(n, 2)
        self.core_copy(j).wait_recv()
        self.part[n] = (self.part[n].astype(f32) + self.core[j].astype(f32)).astype(bf16)

    def rows(self, b):
        return pl.ds(b * self.cut, self.cut)

    def send(self, k, half, b, to, slot):
        copy = remote(
            self.part.at[self.block(k, half), self.rows(b)], self.ring.at[half, slot],
            self.ring_send.at[half, slot], self.ring_recv.at[half, slot], to,
        )
        copy.start()
        self.copies.append(copy)

    def wait(self, half, slot):
        ref = self.ring.at[half, slot]
        remote(ref, ref, self.ring_send.at[half, slot], self.ring_recv.at[half, slot], self.to_core).wait_recv()

    def begin_ring(self, half):
        self.fold_core(2, half)
        self.send(2, half, 0, self.to_left, 0)
        self.send(2, half, 1, self.to_right, 1)
        self.fold_core(1, half)
        self.send(1, half, 0, self.to_right, 2)
        self.fold_core(3, half)
        self.send(3, half, 1, self.to_left, 5)
        self.fold_core(0, half)

    def relay_ring(self, half):
        for k, b, slot, to, target in ((3, 0, 0, self.to_left, 4), (1, 1, 1, self.to_right, 3)):
            self.wait(half, slot)
            n = self.block(k, half)
            total = self.part[n, self.rows(b)].astype(f32) + self.ring[half, slot].astype(f32)
            self.part[n, self.rows(b)] = total.astype(bf16)
            self.send(k, half, b, to, target)

    def ring_total(self, half, b):
        total = self.part[self.block(0, half), self.rows(b)].astype(f32)
        for slot in (2 + b, 4 + b):
            self.wait(half, slot)
            total = total + self.ring[half, slot].astype(f32)
        return total

    def send_half(self):
        n = self.block(0, 0)
        for b in (0, 1):
            self.part[n, self.rows(b)] = self.ring_total(0, b).astype(bf16)
        copy = remote(self.part.at[n], self.half, self.half_send, self.half_recv, self.to_half)
        copy.start()
        self.half_copy = copy

    def result(self):
        totals = [self.ring_total(1, b) for b in (0, 1)]
        self.half_copy.wait_recv()
        return [total + self.half[self.rows(b), :].astype(f32) for b, total in enumerate(totals)]

    def finish(self):
        for copy in self.copies:
            copy.wait_send()
        self.half_copy.wait_send()
        for j in range(8):
            self.core_copy(j).wait_send()


def kernel(
    source_ref, seg_ref, freq_ref, gain_ref, teacher_ref, branch_ref, hidden_ref, q_in, k_in, v_in, att_in, wq_in, wk_in,
    wv_in, w_out_in,
    dh_ref, gq_ref, gk_ref, gv_ref, gout_ref, ggain_ref, hidden_full,
    part, slope, slots, qkv_part, qkv_core, qkv_ring, qkv_half, out_part, out_core, out_ring, out_half,
    att_t, d_att, q_ref, k_ref, v_ref, cos_ref, sin_ref, seg_col, inv_own, inv_all, dk_acc, dv_acc,
    request, sources, gain_sum, gain_block, gain_tensor, gain_dp,
    source_send, source_recv, parcel_send, parcel_recv, hidden_send, hidden_recv, slope_send, slope_recv,
    inv_send, inv_recv, part_send, part_recv,
    qkv_core_send, qkv_core_recv, qkv_ring_send, qkv_ring_recv, qkv_half_send, qkv_half_recv,
    out_core_send, out_core_recv, out_ring_send, out_ring_recv, out_half_send, out_half_recv,
    gain_t_send, gain_t_recv, gain_d_send, gain_d_recv, load_sem, weight_sem, tile_sem,
):
    d, t, x, z = place()
    teacher, branch, own_hidden = part.at[0], part.at[1], part.at[2]
    parcel = [part.at[3], part.at[4]]
    arrived = [part.at[5], part.at[6]]
    dqkv = slope.at[:, :, pl.ds(0, 768)]
    dqkv_t = slope.at[pl.ds(0, 6), :, pl.ds(1024, 1024)]
    kept_hidden = slope.at[pl.ds(0, 4), :, pl.ds(2048, STRIPE)]
    tiles = slope.at[:, :, pl.ds(3072, 512)]

    loads = []

    def load(src, dst):
        copy = pltpu.make_async_copy(src, dst, load_sem.at[len(loads)])
        copy.start()
        loads.append(copy)
        return copy

    load_hidden = load(hidden_ref, own_hidden)
    load_teacher = load(teacher_ref, teacher)
    load_branch = load(branch_ref, branch)

    tensor_peers = [(d, lax.rem(t + k, N_TENSOR)) for k in range(1, N_TENSOR)]
    dp_peers = [(lax.rem(d + k, N_DP), t) for k in range(1, N_DP)]
    hidden_tree = TreeGather(hidden_ref, hidden_full, hidden_send, hidden_recv, 4)
    slope_tree = TreeGather(None, slope, slope_send, slope_recv, 2)
    tree = TreeScatter(part, slots, part_send, part_recv, 3)
    qkv = StageScatter(
        qkv_part, qkv_core, qkv_ring, qkv_half,
        (qkv_core_send, qkv_core_recv, qkv_ring_send, qkv_ring_recv, qkv_half_send.at[0], qkv_half_recv.at[0]),
    )
    out = StageScatter(
        out_part, out_core, out_ring, out_half,
        (out_core_send, out_core_recv, out_ring_send, out_ring_recv, out_half_send.at[0], out_half_recv.at[0]),
    )
    request[...] = jnp.broadcast_to(source_ref[...], (8, ROWS))
    greet(tensor_peers + dp_peers)

    def push_all(peers, src, dst, send, recv):
        copies = [remote(src, dst, send.at[k], recv.at[k], to) for k, to in enumerate(peers)]
        for copy in copies:
            copy.start()
        return copies

    source_copies = push_all(dp_peers, request, sources.at[d], source_send, source_recv)
    hidden_tree.begin()
    sources[d] = request[...]
    load_kept = load(hidden_ref, hidden_full.at[t])
    load_att = [load(att_in.at[pl.ds(s * ROWS, ROWS)], d_att.at[s]) for s in range(8)]
    load_w_out = [
        load(w_out_in.at[:, pl.ds(n * TILE, TILE)], qkv_part.at[n, pl.ds(0, 512)]) for n in range(16)
    ]
    load_qkv = [load(q_in, q_ref), load(k_in, k_ref), load(v_in, v_ref)]

    above = (
        lax.broadcasted_iota(jnp.int32, (ROWS, ROWS), 0) < lax.broadcasted_iota(jnp.int32, (ROWS, ROWS), 1)
    ).astype(bf16)
    slot_ids = lax.broadcasted_iota(jnp.int32, (SLOTS, ROWS), 0)
    peer_ids = lax.broadcasted_iota(jnp.int32, (N_DP, ROWS), 0)
    row_ids = lax.broadcasted_iota(jnp.int32, (ROWS, ROWS), 0)

    def slot_onehot(mask, rank, q):
        return ((slot_ids == rank[q:q + 1]) & (mask[q:q + 1] > 0)).astype(f32).astype(bf16)

    def ranks(mask):
        return jnp.dot(mask.astype(bf16), above, preferred_element_type=f32).astype(jnp.int32)

    from_peer = (peer_ids == lax.shift_right_logical(source_ref[...], 10)).astype(f32)
    from_rank = ranks(from_peer)
    place_rows = jnp.concatenate([slot_onehot(from_peer, from_rank, q) for q in range(N_DP)], axis=0)
    place_rows = place_rows.astype(f32).T.astype(bf16)

    for copy in source_copies:
        copy.wait_recv()
    wanted = jnp.concatenate([sources[q, 0:1, :] for q in range(N_DP)], axis=0)
    mine = (lax.shift_right_logical(wanted, 10) == d).astype(f32)
    rank = ranks(mine)
    local_row = jnp.bitwise_and(wanted, ROWS - 1)
    picks = []
    for q in range(N_DP):
        row_onehot = (row_ids == local_row[q:q + 1]).astype(f32).astype(bf16)
        picks.append(lax.dot_general(slot_onehot(mine, rank, q), row_onehot, NT, preferred_element_type=f32))
    load_teacher.wait()
    for b in (0, 1):
        pick = jnp.concatenate(picks[8 * b:8 * b + 8], axis=0).astype(bf16)
        for n in range(0, D, 512):
            columns = slice(n, n + 512)
            parcel[b][:, columns] = jnp.dot(pick, teacher[:, columns], preferred_element_type=f32).astype(bf16)

    def slot_rows(first, q):
        return part.at[first + lax.div(q, 8), pl.ds(pl.multiple_of(lax.rem(q, 8) * SLOTS, SLOTS), SLOTS)]

    parcel_copies = []
    for k, to in enumerate(dp_peers):
        copy = remote(slot_rows(3, to[0]), slot_rows(5, d), parcel_send.at[k], parcel_recv.at[k], to)
        copy.start()
        parcel_copies.append(copy)
    keep_own = load(slot_rows(3, d), slot_rows(5, d))

    load_hidden.wait()
    squares = jnp.zeros((ROWS, 128), f32)
    for n in range(0, D, 128):
        values = own_hidden[:, n:n + 128].astype(f32)
        squares = squares + values * values
    inv_rms = lax.rsqrt(jnp.sum(squares, axis=1, keepdims=True) * (1.0 / D) + eps_norm)
    inv_own[...] = jnp.broadcast_to(inv_rms, (ROWS, 128))
    inv_copies = push_all(tensor_peers, inv_own, inv_all.at[t], inv_send, inv_recv)
    inv_all[t] = inv_own[...]

    hidden_steps = hidden_tree.steps()
    for step in hidden_steps[:2]:
        step()

    seg_row = seg_ref[...].astype(f32)
    before = jnp.zeros_like(seg_row)
    for value in range(3):
        count = jnp.sum((seg_row == value).astype(f32), axis=1, keepdims=True)
        before = before + jnp.where(seg_row > value, count, 0.0)
    positions = lax.broadcasted_iota(jnp.int32, (1, GROUP), 1).astype(f32) - before
    for n in range(0, GROUP, 128):
        angles = freq_ref[...] * positions[:, n:n + 128]
        cos_ref[:, n:n + 128] = jnp.cos(angles)
        sin_ref[:, n:n + 128] = jnp.sin(angles)
    seg_col[...] = jnp.broadcast_to(seg_row, (128, GROUP)).T

    for step in hidden_steps[2:6]:
        step()
    for copy in load_att:
        copy.wait()
    for e in (0, 1):
        rows = jnp.concatenate([d_att[2 * i + e] for i in range(4)], axis=0)
        att_t[e] = rows.astype(f32).T.astype(bf16)
    for step in hidden_steps[6:8]:
        step()

    keep_own.wait()
    load_branch.wait()
    for copy in parcel_copies:
        copy.wait_recv()
    for n in range(0, D, 512):
        columns = slice(n, n + 512)
        target = jnp.dot(place_rows[:, :128], arrived[0][:, columns], preferred_element_type=f32)
        target += jnp.dot(place_rows[:, 128:], arrived[1][:, columns], preferred_element_type=f32)
        slope[t, :, columns] = ((branch[:, columns].astype(f32) - target) * (N_DP * GROUP) ** -0.5).astype(bf16)
    slope_tree.begin()
    slope_steps = slope_tree.steps()
    for step in hidden_steps[8:12] + slope_steps[:2] + hidden_steps[12:16] + slope_steps[2:8] + hidden_steps[16:20]:
        step()

    for step in slope_steps[8:18]:
        step()
    for copy in load_w_out:
        copy.wait()

    def slope_rows(e, columns):
        return jnp.concatenate([slope[2 * i + e, :, columns] for i in range(4)], axis=0)

    def attended_slope(e):
        def tile(n, carry):
            heads = pl.ds(pl.multiple_of(n * 256, 256), 256)
            value = jnp.zeros((512, 256), f32)
            for k in range(16):
                rows = slope_rows(e, slice(k * TILE, (k + 1) * TILE))
                value += lax.dot_general(rows, qkv_part[k, heads, :], NT, preferred_element_type=f32)
            value = value.astype(bf16)
            for i in range(4):
                d_att[2 * i + e, :, heads] = value[i * ROWS:(i + 1) * ROWS]
            return carry

        lax.fori_loop(0, 2, tile, 0)

    def out_gradient(e, first):
        def tile(n, carry):
            columns = pl.ds(pl.multiple_of(n * TILE, TILE), TILE)
            value = jnp.dot(att_t[e], slope_rows(e, columns), preferred_element_type=f32)
            if not first:
                value = value + out_part[n].astype(f32)
            out_part[n] = value.astype(bf16)
            return carry

        return tile

    attended_slope(z)
    lax.fori_loop(0, 16, out_gradient(z, True), 0)
    for step in slope_steps[18:]:
        step()
    attended_slope(1 - z)
    weight_copies = []
    for n in range(16):
        rows = pl.ds(n * TILE, TILE)
        for i, (src, dst) in enumerate((
            (wq_in.at[rows, pl.ds(0, 256)], qkv_part.at[n, pl.ds(0, 256)]),
            (wq_in.at[rows, pl.ds(256, 256)], qkv_part.at[n, pl.ds(256, 256)]),
            (wk_in.at[rows], qkv_part.at[n, pl.ds(512, 256), pl.ds(0, 128)]),
            (wv_in.at[rows], qkv_part.at[n, pl.ds(512, 256), pl.ds(128, 128)]),
        )):
            copy = pltpu.make_async_copy(src, dst, weight_sem.at[n, i])
            copy.start()
            weight_copies.append(copy)
    slope_tree.finish()
    lax.fori_loop(0, 16, out_gradient(1 - z, False), 0)
    for j in range(8):
        out.core_copy(j).start()
    for p in range(4):
        load(hidden_ref.at[:, pl.ds(p * STRIPE, STRIPE)], kept_hidden.at[p])

    for copy in load_qkv:
        copy.wait()
    blk = 256
    scale = HD ** -0.5
    dk_acc[...] = jnp.zeros_like(dk_acc)
    dv_acc[...] = jnp.zeros_like(dv_acc)
    k_t = k_ref[...].astype(f32).T.astype(bf16)

    def rotate_back(values, columns):
        u, w = values[:64], values[64:]
        c, s = cos_ref[:, columns], sin_ref[:, columns]
        return jnp.concatenate([u * c + w * s, w * c - u * s], axis=0)

    for i in range(GROUP // blk):
        rows = slice(i * blk, (i + 1) * blk)
        seen = (i + 1) * blk
        keys = jnp.concatenate([seg_col[:seen, :]] * 2, axis=1)
        allowed = (keys == seg_row[:, rows]) & (
            lax.broadcasted_iota(jnp.int32, (seen, blk), 0) <= lax.broadcasted_iota(jnp.int32, (seen, blk), 1) + i * blk
        )
        for h in range(4):
            cols = slice(h * HD, (h + 1) * HD)
            q = q_ref[rows, cols]
            da = d_att[2 * i:2 * i + 2, :, cols].reshape(blk, HD)
            scores = lax.dot_general(k_ref[:seen, :], q, NT, preferred_element_type=f32) * scale
            scores = jnp.where(allowed, scores, -1e30)
            weights = jnp.where(allowed, jnp.exp(scores - jnp.max(scores, axis=0, keepdims=True)), 0.0)
            soft = weights * (1.0 / jnp.sum(weights, axis=0, keepdims=True))
            d_probs = lax.dot_general(v_ref[:seen, :], da, NT, preferred_element_type=f32)
            delta = jnp.sum(soft * d_probs, axis=0, keepdims=True)
            d_scores = (soft * (d_probs - delta) * scale).astype(bf16)
            dv_acc[:seen, :] += jnp.dot(soft.astype(bf16), da, preferred_element_type=f32)
            dk_acc[:seen, :] += jnp.dot(d_scores, q, preferred_element_type=f32)
            dq_t = rotate_back(jnp.dot(k_t[:, :seen], d_scores, preferred_element_type=f32), rows)
            dqkv_t[h, :, rows] = dq_t.astype(bf16)
            dqkv[2 * i:2 * i + 2, :, cols] = dq_t.T.astype(bf16).reshape(2, ROWS, HD)
        if i == 1:
            out.begin_ring(0)
            out.begin_ring(1)
    dk_t = rotate_back(dk_acc[...].T, slice(0, GROUP))
    dqkv_t[4] = dk_t.astype(bf16)
    dqkv[:, :, 512:640] = dk_t.T.astype(bf16).reshape(8, ROWS, HD)
    dqkv_t[5] = dv_acc[...].T.astype(bf16)
    dqkv[:, :, 640:768] = dv_acc[...].astype(bf16).reshape(8, ROWS, HD)
    out.relay_ring(0)
    out.relay_ring(1)

    for copy in parcel_copies:
        copy.wait_send()
    for step in hidden_steps[20:]:
        step()
    for copy in inv_copies:
        copy.wait_recv()
    load_kept.wait()
    for copy in weight_copies:
        copy.wait()

    def tile_copy(n, slot):
        columns = pl.ds(pl.multiple_of(n * TILE, TILE), TILE)
        return pltpu.make_async_copy(hidden_full.at[:, :, columns], tiles.at[:, :, pl.ds(pl.multiple_of(slot * TILE, TILE), TILE)], tile_sem.at[slot])

    order = (0, 3, 1, 2)
    tile_copy(4 * order[0], 0).start()
    for g, p in enumerate(order):
        following = order[g + 1] if g < 3 else None

        def tile(i, carry, p=p, following=following):
            n = 4 * p + i
            slot = lax.rem(i, 2)
            if following is None:
                @pl.when(i < 3)
                def _():
                    tile_copy(n + 1, 1 - slot).start()
            else:
                tile_copy(n + 1 + lax.div(i + 1, 4) * (4 * (following - p) - 4), 1 - slot).start()
            tile_copy(n, slot).wait()
            columns = pl.ds(pl.multiple_of(n * TILE, TILE), TILE)
            inv = inv_all[...].reshape(GROUP, 128)
            held = tiles[:, :, pl.ds(pl.multiple_of(slot * TILE, TILE), TILE)]
            unit = held.reshape(GROUP, TILE).astype(f32) * jnp.concatenate([inv, inv], axis=1)
            normed = (unit * gain_ref[:, columns]).astype(bf16)
            grads = dqkv[...].reshape(GROUP, 768)
            total = lax.dot_general(grads[:, :256], qkv_part[n, :256, :], NT, preferred_element_type=f32)
            total += lax.dot_general(grads[:, 256:512], qkv_part[n, 256:512, :], NT, preferred_element_type=f32)
            total += lax.dot_general(grads[:, 512:], qkv_part[n, 512:, :], NT, preferred_element_type=f32)
            part[:, :, columns] = total.astype(bf16).reshape(8, ROWS, TILE)
            gain_sum[:, columns] = jnp.sum((total * unit).reshape(ROWS, 8, TILE), axis=0)
            qkv_part[n] = jnp.dot(
                dqkv_t[...].reshape(768, GROUP), normed, preferred_element_type=f32
            ).astype(bf16)
            return carry

        lax.fori_loop(0, 4, tile, 0)
        if p >= tree.over_z:
            tree.begin_z(p)
        else:
            tree.begin_x(1, p)
            tree.begin_x(0, p)
        qkv.core_copy(2 * p).start()
        qkv.core_copy(2 * p + 1).start()

    gain_row = jnp.sum(gain_sum[...], axis=0, keepdims=True)
    for i in range(32):
        gain_block[0, i:i + 1, :] = gain_row[:, i * 128:(i + 1) * 128]
    gain_tensor[t] = gain_block[0]
    gain_copies = push_all(tensor_peers, gain_block.at[0], gain_tensor.at[t], gain_t_send, gain_t_recv)

    tree.relay(1, 0)
    tree.relay(0, 0)
    qkv.begin_ring(0)
    qkv.begin_ring(1)
    tree.relay(1, 1)
    tree.relay(0, 1)
    tree.z_done(2, 3)
    tree.z_done(3, 3)
    tree.begin_x(0, 3)
    qkv.relay_ring(0)
    tree.root_other(0)
    tree.relay(1, 2)
    tree.relay(0, 2)
    qkv.relay_ring(1)
    tree.z_done(1, 3)
    tree.root_other(1)
    out.send_half()

    for copy in gain_copies:
        copy.wait_recv()
    gain_total = gain_tensor[0]
    for k in range(1, N_TENSOR):
        gain_total = gain_total + gain_tensor[k]
    gain_block[1] = gain_total
    gain_dp[d] = gain_total
    dp_copies = push_all(dp_peers, gain_block.at[1], gain_dp.at[d], gain_d_send, gain_d_recv)

    tree.relay(0, 3)
    tree.z_done(0, 3)
    tree.root_other(2)
    qkv.send_half()
    for b, value in enumerate(out.result()):
        gout_ref[b * 256:(b + 1) * 256, :] = value

    for copy in dp_copies:
        copy.wait_recv()
    gain_total = gain_dp[0]
    for k in range(1, N_DP):
        gain_total = gain_total + gain_dp[k]
    ggain_ref[...] = gain_total

    for copy in loads[-4:]:
        copy.wait()
    inv = inv_own[:, 0:1]
    dots = jnp.zeros((ROWS, 1), f32)
    for p in (0, 1, 3, 2):
        columns = slice(p * STRIPE, (p + 1) * STRIPE)
        scaled = tree.result(p) * gain_ref[:, columns]
        dh_ref[:, columns] = scaled
        unit = kept_hidden[p].astype(f32) * inv
        dots = dots + jnp.sum(scaled * unit, axis=1, keepdims=True)
    mean = dots * (1.0 / D)
    for p in range(4):
        columns = slice(p * STRIPE, (p + 1) * STRIPE)
        unit = kept_hidden[p].astype(f32) * inv
        dh_ref[:, columns] = inv * (dh_ref[:, columns] - unit * mean)
    top, bottom = qkv.result()
    gq_ref[:, :384] = top.T
    gq_ref[:, 384:] = bottom[:128].T
    gk_ref[...] = bottom[128:256].T
    gv_ref[...] = bottom[256:].T

    hidden_tree.finish()
    tree.finish()
    out.finish()
    qkv.finish()
    for copy in source_copies + inv_copies + gain_copies + dp_copies:
        copy.wait_send()


def per_device(
    hidden_in, teacher, row_source, segments, branch, queries, key_rot, value_rows, attended, norm_gain,
    w_query, w_key, w_value, w_out,
):
    any_space = pl.BlockSpec(memory_space=pl.ANY)
    vmem = pl.BlockSpec(memory_space=pltpu.VMEM)
    dma = pltpu.SemaphoreType.DMA
    scratch = pltpu.VMEM
    frequency = (theta_base ** (-2.0 * np.arange(HD // 2, dtype=np.float64) / HD)).astype(np.float32)
    frequency = np.broadcast_to(frequency[:, None], (HD // 2, 128))
    stage_sems = [dma((8,)), dma((8,)), dma((2, 6)), dma((2, 6)), dma((1,)), dma((1,))]
    shape = jax.ShapeDtypeStruct
    d_hidden, grad_query, grad_key, grad_value, grad_out, grad_gain, _ = pl.pallas_call(
        kernel,
        out_shape=(
            shape((ROWS, D), f32), shape((256, 512), f32), shape((256, 128), f32), shape((256, 128), f32),
            shape((512, 256), f32), shape((32, 128), f32), shape((N_TENSOR, ROWS, D), bf16),
        ),
        in_specs=[vmem] * 4 + [any_space] * 11,
        out_specs=(vmem,) * 6 + (any_space,),
        scratch_shapes=[
            scratch((8, ROWS, D), bf16), scratch((8, ROWS, D), bf16), scratch((28, ROWS, STRIPE), bf16),
            scratch((16, 768, 256), bf16), scratch((8, 768, 256), bf16), scratch((2, 6, 384, 256), bf16), scratch((768, 256), bf16),
            scratch((16, 512, 256), bf16), scratch((8, 512, 256), bf16), scratch((2, 6, 256, 256), bf16), scratch((512, 256), bf16),
            scratch((2, 512, 512), bf16), scratch((8, ROWS, 512), bf16),
            scratch((GROUP, 512), bf16), scratch((GROUP, HD), bf16), scratch((GROUP, HD), bf16),
            scratch((HD // 2, GROUP), f32), scratch((HD // 2, GROUP), f32), scratch((GROUP, 128), f32),
            scratch((ROWS, 128), f32), scratch((N_TENSOR, ROWS, 128), f32),
            scratch((GROUP, HD), f32), scratch((GROUP, HD), f32),
            scratch((8, ROWS), jnp.int32), scratch((N_DP, 8, ROWS), jnp.int32),
            scratch((8, D), f32), scratch((2, 32, 128), f32), scratch((N_TENSOR, 32, 128), f32), scratch((N_DP, 32, 128), f32),
            dma((15,)), dma((15,)), dma((15,)), dma((15,)),
            dma((28,)), dma((8, 4)), dma((28,)), dma((8, 4)),
            dma((7,)), dma((7,)), dma((28,)), dma((28,)),
        ] + stage_sems + stage_sems + [
            dma((7,)), dma((7,)), dma((15,)), dma((15,)), dma((40,)), dma((16, 4)), dma((2,)),
        ],
        compiler_params=pltpu.CompilerParams(
            collective_id=1, has_side_effects=True, vmem_limit_bytes=60 * 2**20
        ),
        cost_estimate=pl.CostEstimate(flops=27 * 10**9, bytes_accessed=60 * 2**20, transcendentals=4 * 2**20),
    )(
        row_source[None, :], segments, frequency, norm_gain[None, :], teacher, branch, hidden_in, queries, key_rot, value_rows,
        attended, w_query, w_key, w_value, w_out,
    )
    return (grad_query, grad_key, grad_value, grad_out, grad_gain.reshape(D), d_hidden)


def solution(mesh):
    return jax.shard_map(
        per_device,
        mesh=mesh,
        in_specs=(
            P(("dp", "tensor"), None),
            P(("dp", "tensor"), None),
            P(("dp", "tensor")),
            P("dp", None),
            P(("dp", "tensor"), None),
            P("dp", "tensor"),
            P("dp", "tensor"),
            P("dp", "tensor"),
            P("dp", "tensor"),
            P(),
            P(None, "tensor"),
            P(None, "tensor"),
            P(None, "tensor"),
            P("tensor", None),
        ),
        out_specs=(
            P("dp", "tensor"),
            P("dp", "tensor"),
            P("dp", "tensor"),
            P("tensor", "dp"),
            P(),
            P(("dp", "tensor"), None),
        ),
        check_vma=False,
    )
```

time: 999 us -> 263 us (0.26)
  waiting for transfers between devices: 706 us -> 0 us
  Pallas kernels: 0 us -> 249 us
  matrix products: 111 us -> 0 us
  blocking collectives: 81.5 us -> 0 us
  other arithmetic: 52.6 us -> 0 us
  between operations: 14.7 us -> 0.64 us
  local copies, waits for them, and re-layouts: 23.1 us -> 12.7 us
    reduce_scatter x5 -> x0, waiting for transfers between devices: 393 us -> none  [the longest x1 168 us: per_device(): lax.psum_scatter((total + lax.dot_general(d_value, w_value, contract_cols...]
    all_gather x2 -> x0, waiting for transfers between devices: 271 us -> none  [the longest x1 170 us: per_device(): full_slope = lax.all_gather(out_slope, 'tensor', axis=0, tiled=True)]
    pallas_call x0 -> x1, Pallas kernels: none -> 249 us  [per_device(): pl.pallas_call(kernel, out_shape=(shape((ROWS, D), f32), shape((256, 512)...]
    dot_general x13 -> x0, matrix products: 111 us -> none  [the longest x1 15.4 us: per_device(): lax.dot_general(d_value, w_value, contract_cols, preferred_element_type=f32)]
    psum x1 -> x0, blocking collectives: 66.2 us -> none  [per_device(): grad_gain = lax.psum(gain_part, ('dp', 'tensor'))]
    all_to_all x1 -> x0, waiting for transfers between devices: 40.9 us -> none  [relay_teacher(): lax.all_to_all(parcel, 'dp', split_axis=0, concat_axis=0, tiled=True)]
    mul x2 -> x0, other arithmetic: 15.6 us -> none  [the longest x1 11.9 us: per_device(): unit_rows = floated * inv_rms]
    all_to_all x1 -> x0, blocking collectives: 15.3 us -> none  [relay_teacher(): lax.all_to_all(request, 'dp', split_axis=0, concat_axis=0, tiled=True)]
  transfers between devices with their start and end apart: 8 -> 0, of which waited for: 7 -> 0; matrix products, arithmetic and copies ran while one was open for 12% -> 0% of each run, Pallas kernels for 0% -> 0%
where the time goes in v2:
time: 263 us; the launch traced here: 262 us
  Pallas kernels  249 us (95%)
  local copies, waits for them, and re-layouts  12.7 us (5%)
    pallas_call x1, Pallas kernels, per_device(): pl.pallas_call(kernel, out_shape=(shape((ROWS, D), f32), shape((256, 512)...  249 us
    unnamed x6, local copies, waits for them, and re-layouts  11.3 us

profile of v2, /device:TPU:0, one launch (start us, length us, event | category | flops | bytes accessed | tf_op | source)
XLA Modules:
  0.0 262.0 jit_solution(3541947967768059211)
XLA Ops:
  0.6 1.3 jit_solution_.3.freq_ref
  2.0 248.7 %shard_map.190 = (f32[128,4096]{1,0:T(8,128)}, f32[256,512]{1,0:T(8,128)}, f32[256,128]{1,0:T(8,128)}, f32[256,128]{1,0:T(8,128)}, f32[512,256]{1,0:T(8,128)}, /...) custom-call(s32[1,128]{1,0:T(1,128)} %bitcast.5, s32[1,1024]{1,0:T(1,128)} %seg_ref.1, f32[64,128]{1,0:T(8,128)} %jit_solution_.3.freq_ref, ...), custom_call_target="tpu_custom_call" | custom-call | flops 27000000512 | bytes 62914560 | tf_op jit(solution)/shard_map/pallas_call | solution.py:712
  250.7 1.9 copy.27
  252.6 1.6 copy.28
  254.2 1.6 copy.29
  255.7 1.9 copy.30
  257.6 1.3 copy.31
  258.9 3.1 %copy.32 = f32[128,4096]{1,0:T(8,128)} copy(f32[128,4096]{1,0:T(8,128)} %get-tuple-element.29) | data formatting | bytes 4194304

commit v3 on v2

--- a/solution.py
+++ b/solution.py
@@ -14,7 +14,9 @@
 GROUP = 1024
 N_DP = 16
 N_TENSOR = 8
-SLOTS = 16
+CAPACITY = 9
+CHUNK = 512
+SLOTS = 80
 PIECE = 32
 STRIPE = 1024
 TILE = 256
@@ -121,7 +123,11 @@
                     self.send(s, p, to)
             return step
 
-        return [make(*entry) for entry in plan]
+        roles = {id(s): name for s, name in (
+            (partner, "partner"), (left, "left"), (right, "right"), (across, "across"),
+            (far_left, "far_left"), (far_right, "far_right"), (far_across, "far_across"),
+        )}
+        return {(roles[id(s)], p): make(s, p, targets) for s, p, targets in plan}
 
     def finish(self):
         for copy in self.copies:
@@ -232,8 +238,7 @@
         )
 
     def block(self, k, half):
-        zh = 1 - self.zh if half == 0 else self.zh
-        return 2 * (zh * 4 + lax.rem(self.y + k, 4)) + self.c
+        return 2 * (half * 4 + lax.rem(self.y + k, 4)) + self.c
 
     def fold_core(self, k, half):
         n = self.block(k, half)
@@ -282,15 +287,15 @@
         return total
 
     def send_half(self):
-        n = self.block(0, 0)
+        n = self.block(0, 1 - self.zh)
         for b in (0, 1):
-            self.part[n, self.rows(b)] = self.ring_total(0, b).astype(bf16)
+            self.part[n, self.rows(b)] = self.ring_total(1 - self.zh, b).astype(bf16)
         copy = remote(self.part.at[n], self.half, self.half_send, self.half_recv, self.to_half)
         copy.start()
         self.half_copy = copy
 
     def result(self):
-        totals = [self.ring_total(1, b) for b in (0, 1)]
+        totals = [self.ring_total(self.zh, b) for b in (0, 1)]
         self.half_copy.wait_recv()
         return [total + self.half[self.rows(b), :].astype(f32) for b, total in enumerate(totals)]
 
@@ -303,7 +308,7 @@
 
 
 def kernel(
-    source_ref, seg_ref, freq_ref, gain_ref, teacher_ref, branch_ref, hidden_ref, q_in, k_in, v_in, att_in, wq_in, wk_in,
+    source_ref, seg_ref, gain_ref, teacher_ref, branch_ref, hidden_ref, q_in, k_in, v_in, att_in, wq_in, wk_in,
     wv_in, w_out_in,
     dh_ref, gq_ref, gk_ref, gv_ref, gout_ref, ggain_ref, hidden_full,
     part, slope, slots, qkv_part, qkv_core, qkv_ring, qkv_half, out_part, out_core, out_ring, out_half,
@@ -317,8 +322,6 @@
 ):
     d, t, x, z = place()
     teacher, branch, own_hidden = part.at[0], part.at[1], part.at[2]
-    parcel = [part.at[3], part.at[4]]
-    arrived = [part.at[5], part.at[6]]
     dqkv = slope.at[:, :, pl.ds(0, 768)]
     dqkv_t = slope.at[pl.ds(0, 6), :, pl.ds(1024, 1024)]
     kept_hidden = slope.at[pl.ds(0, 4), :, pl.ds(2048, STRIPE)]
@@ -338,7 +341,7 @@
 
     tensor_peers = [(d, lax.rem(t + k, N_TENSOR)) for k in range(1, N_TENSOR)]
     dp_peers = [(lax.rem(d + k, N_DP), t) for k in range(1, N_DP)]
-    hidden_tree = TreeGather(hidden_ref, hidden_full, hidden_send, hidden_recv, 4)
+    hidden_tree = TreeGather(hidden_ref, hidden_full, hidden_send, hidden_recv, 3)
     slope_tree = TreeGather(None, slope, slope_send, slope_recv, 2)
     tree = TreeScatter(part, slots, part_send, part_recv, 3)
     qkv = StageScatter(
@@ -361,7 +364,6 @@
     source_copies = push_all(dp_peers, request, sources.at[d], source_send, source_recv)
     hidden_tree.begin()
     sources[d] = request[...]
-    load_kept = load(hidden_ref, hidden_full.at[t])
     load_att = [load(att_in.at[pl.ds(s * ROWS, ROWS)], d_att.at[s]) for s in range(8)]
     load_w_out = [
         load(w_out_in.at[:, pl.ds(n * TILE, TILE)], qkv_part.at[n, pl.ds(0, 512)]) for n in range(16)
@@ -371,7 +373,9 @@
     above = (
         lax.broadcasted_iota(jnp.int32, (ROWS, ROWS), 0) < lax.broadcasted_iota(jnp.int32, (ROWS, ROWS), 1)
     ).astype(bf16)
-    slot_ids = lax.broadcasted_iota(jnp.int32, (SLOTS, ROWS), 0)
+    block_row = lax.broadcasted_iota(jnp.int32, (SLOTS, ROWS), 0)
+    chunk_ids = lax.shift_right_logical(block_row * 57, 9)
+    slot_ids = block_row - CAPACITY * chunk_ids
     peer_ids = lax.broadcasted_iota(jnp.int32, (N_DP, ROWS), 0)
     row_ids = lax.broadcasted_iota(jnp.int32, (ROWS, ROWS), 0)
 
@@ -382,9 +386,13 @@
         return jnp.dot(mask.astype(bf16), above, preferred_element_type=f32).astype(jnp.int32)
 
     from_peer = (peer_ids == lax.shift_right_logical(source_ref[...], 10)).astype(f32)
-    from_rank = ranks(from_peer)
-    place_rows = jnp.concatenate([slot_onehot(from_peer, from_rank, q) for q in range(N_DP)], axis=0)
-    place_rows = place_rows.astype(f32).T.astype(bf16)
+    taken = jnp.sum(from_peer * (SLOTS * peer_ids + ranks(from_peer)).astype(f32), axis=0, keepdims=True)
+    taken = jnp.concatenate([jnp.broadcast_to(taken, (ROWS, ROWS)).T] * 10, axis=1)
+    lanes = lax.broadcasted_iota(jnp.int32, (ROWS, N_DP * SLOTS), 1).astype(f32)
+    for k in range(8):
+        onehot = (lanes == taken + CAPACITY * k).astype(f32).astype(bf16)
+        for n in range(5):
+            out_part[2 * n + k // 4, (k % 4) * ROWS:(k % 4 + 1) * ROWS, :] = onehot[:, n * TILE:(n + 1) * TILE]
 
     for copy in source_copies:
         copy.wait_recv()
@@ -397,14 +405,20 @@
         row_onehot = (row_ids == local_row[q:q + 1]).astype(f32).astype(bf16)
         picks.append(lax.dot_general(slot_onehot(mine, rank, q), row_onehot, NT, preferred_element_type=f32))
     load_teacher.wait()
-    for b in (0, 1):
-        pick = jnp.concatenate(picks[8 * b:8 * b + 8], axis=0).astype(bf16)
-        for n in range(0, D, 512):
-            columns = slice(n, n + 512)
-            parcel[b][:, columns] = jnp.dot(pick, teacher[:, columns], preferred_element_type=f32).astype(bf16)
+    chunks = jnp.concatenate([teacher[:, k * CHUNK:(k + 1) * CHUNK] for k in range(8)], axis=0)
+    for b in range(4):
+        pick = jnp.concatenate([
+            jnp.concatenate([jnp.where(chunk_ids == k, picks[q], 0.0).astype(bf16) for k in range(8)], axis=1)
+            for q in range(4 * b, 4 * b + 4)
+        ], axis=0)
+        values = jnp.dot(pick, chunks, preferred_element_type=f32).astype(bf16)
+        for i in range(4):
+            q = 4 * b + i
+            part[3 + q // 8, :SLOTS, (q % 8) * CHUNK:(q % 8 + 1) * CHUNK] = values[i * SLOTS:(i + 1) * SLOTS]
 
     def slot_rows(first, q):
-        return part.at[first + lax.div(q, 8), pl.ds(pl.multiple_of(lax.rem(q, 8) * SLOTS, SLOTS), SLOTS)]
+        columns = pl.ds(pl.multiple_of(lax.rem(q, 8) * CHUNK, CHUNK), CHUNK)
+        return part.at[first + lax.div(q, 8), pl.ds(0, SLOTS), columns]
 
     parcel_copies = []
     for k, to in enumerate(dp_peers):
@@ -414,6 +428,7 @@
     keep_own = load(slot_rows(3, d), slot_rows(5, d))
 
     load_hidden.wait()
+    load_kept = load(own_hidden, hidden_full.at[t])
     squares = jnp.zeros((ROWS, 128), f32)
     for n in range(0, D, 128):
         values = own_hidden[:, n:n + 128].astype(f32)
@@ -424,8 +439,13 @@
     inv_all[t] = inv_own[...]
 
     hidden_steps = hidden_tree.steps()
-    for step in hidden_steps[:2]:
-        step()
+    slope_steps = slope_tree.steps()
+
+    def take(steps, *names):
+        for role, p in names:
+            steps.pop((role, p))()
+
+    take(hidden_steps, ("partner", 0), ("left", 3), ("right", 3), ("left", 0))
 
     seg_row = seg_ref[...].astype(f32)
     before = jnp.zeros_like(seg_row)
@@ -433,38 +453,77 @@
         count = jnp.sum((seg_row == value).astype(f32), axis=1, keepdims=True)
         before = before + jnp.where(seg_row > value, count, 0.0)
     positions = lax.broadcasted_iota(jnp.int32, (1, GROUP), 1).astype(f32) - before
+    steps_down = lax.broadcasted_iota(jnp.int32, (HD // 2, 128), 0).astype(f32)
+    frequency = jnp.exp(steps_down * float(-2.0 * np.log(theta_base) / HD))
     for n in range(0, GROUP, 128):
-        angles = freq_ref[...] * positions[:, n:n + 128]
+        angles = frequency * positions[:, n:n + 128]
         cos_ref[:, n:n + 128] = jnp.cos(angles)
         sin_ref[:, n:n + 128] = jnp.sin(angles)
     seg_col[...] = jnp.broadcast_to(seg_row, (128, GROUP)).T
 
-    for step in hidden_steps[2:6]:
-        step()
+    take(hidden_steps, ("partner", 1), ("right", 1))
     for copy in load_att:
         copy.wait()
     for e in (0, 1):
         rows = jnp.concatenate([d_att[2 * i + e] for i in range(4)], axis=0)
         att_t[e] = rows.astype(f32).T.astype(bf16)
-    for step in hidden_steps[6:8]:
-        step()
+    take(hidden_steps, ("left", 2))
 
     keep_own.wait()
     load_branch.wait()
     for copy in parcel_copies:
         copy.wait_recv()
-    for n in range(0, D, 512):
-        columns = slice(n, n + 512)
-        target = jnp.dot(place_rows[:, :128], arrived[0][:, columns], preferred_element_type=f32)
-        target += jnp.dot(place_rows[:, 128:], arrived[1][:, columns], preferred_element_type=f32)
-        slope[t, :, columns] = ((branch[:, columns].astype(f32) - target) * (N_DP * GROUP) ** -0.5).astype(bf16)
+    came = jnp.concatenate(
+        [part[5 + q // 8, :SLOTS, (q % 8) * CHUNK:(q % 8 + 1) * CHUNK] for q in range(N_DP)], axis=0
+    )
+    for b in (0, 1):
+        onehot = jnp.concatenate([out_part[2 * n + b] for n in range(5)], axis=1)
+        target = jnp.dot(onehot, came, preferred_element_type=f32)
+        for i in range(4):
+            columns = slice((4 * b + i) * CHUNK, (4 * b + i + 1) * CHUNK)
+            change = branch[:, columns].astype(f32) - target[i * ROWS:(i + 1) * ROWS]
+            slope[t, :, columns] = (change * (N_DP * GROUP) ** -0.5).astype(bf16)
     slope_tree.begin()
-    slope_steps = slope_tree.steps()
-    for step in hidden_steps[8:12] + slope_steps[:2] + hidden_steps[12:16] + slope_steps[2:8] + hidden_steps[16:20]:
-        step()
-
-    for step in slope_steps[8:18]:
-        step()
+    for copy in parcel_copies:
+        copy.wait_send()
+
+    for copy in load_qkv:
+        copy.wait()
+    blk = 256
+    scale = HD ** -0.5
+
+    def forward(i):
+        rows = slice(i * blk, (i + 1) * blk)
+        seen = (i + 1) * blk
+        keys = jnp.concatenate([seg_col[:seen, :]] * 2, axis=1)
+        allowed = (keys == seg_row[:, rows]) & (
+            lax.broadcasted_iota(jnp.int32, (seen, blk), 0) <= lax.broadcasted_iota(jnp.int32, (seen, blk), 1) + i * blk
+        )
+        for h in range(4):
+            scores = lax.dot_general(
+                k_ref[:seen, :], q_ref[rows, h * HD:(h + 1) * HD], NT, preferred_element_type=f32
+            ) * scale
+            scores = jnp.where(allowed, scores, -1e30)
+            weights = jnp.where(allowed, jnp.exp(scores - jnp.max(scores, axis=0, keepdims=True)), 0.0)
+            soft = (weights * (1.0 / jnp.sum(weights, axis=0, keepdims=True))).astype(bf16)
+            first = (4 * i + h) * blk
+            part[:2 * (i + 1), :, first:first + blk] = soft.reshape(2 * (i + 1), ROWS, blk)
+
+    load_kept.wait()
+    take(hidden_steps, ("far_left", 0), ("far_right", 1), ("across", 3))
+    forward(0)
+    take(slope_steps, ("partner", 0), ("partner", 1))
+    forward(1)
+    take(slope_steps, ("left", 2), ("right", 3), ("left", 3), ("right", 2))
+    forward(2)
+    take(slope_steps, ("left", 0), ("right", 1))
+    take(hidden_steps, ("partner", 2))
+    take(slope_steps, ("far_left", 0), ("far_right", 1))
+    forward(3)
+
+    for p in (2, 3, 0, 1):
+        take(slope_steps, ("across", p))
+    take(slope_steps, ("left", 1), ("right", 0))
     for copy in load_w_out:
         copy.wait()
 
@@ -498,7 +557,8 @@
 
     attended_slope(z)
     lax.fori_loop(0, 16, out_gradient(z, True), 0)
-    for step in slope_steps[18:]:
+    take(hidden_steps, ("far_left", 2))
+    for step in slope_steps.values():
         step()
     attended_slope(1 - z)
     weight_copies = []
@@ -520,10 +580,6 @@
     for p in range(4):
         load(hidden_ref.at[:, pl.ds(p * STRIPE, STRIPE)], kept_hidden.at[p])
 
-    for copy in load_qkv:
-        copy.wait()
-    blk = 256
-    scale = HD ** -0.5
     dk_acc[...] = jnp.zeros_like(dk_acc)
     dv_acc[...] = jnp.zeros_like(dv_acc)
     k_t = k_ref[...].astype(f32).T.astype(bf16)
@@ -536,22 +592,17 @@
     for i in range(GROUP // blk):
         rows = slice(i * blk, (i + 1) * blk)
         seen = (i + 1) * blk
-        keys = jnp.concatenate([seg_col[:seen, :]] * 2, axis=1)
-        allowed = (keys == seg_row[:, rows]) & (
-            lax.broadcasted_iota(jnp.int32, (seen, blk), 0) <= lax.broadcasted_iota(jnp.int32, (seen, blk), 1) + i * blk
-        )
         for h in range(4):
             cols = slice(h * HD, (h + 1) * HD)
             q = q_ref[rows, cols]
             da = d_att[2 * i:2 * i + 2, :, cols].reshape(blk, HD)
-            scores = lax.dot_general(k_ref[:seen, :], q, NT, preferred_element_type=f32) * scale
-            scores = jnp.where(allowed, scores, -1e30)
-            weights = jnp.where(allowed, jnp.exp(scores - jnp.max(scores, axis=0, keepdims=True)), 0.0)
-            soft = weights * (1.0 / jnp.sum(weights, axis=0, keepdims=True))
+            first = (4 * i + h) * blk
+            probs = part[:2 * (i + 1), :, first:first + blk].reshape(seen, blk)
+            soft = probs.astype(f32)
             d_probs = lax.dot_general(v_ref[:seen, :], da, NT, preferred_element_type=f32)
             delta = jnp.sum(soft * d_probs, axis=0, keepdims=True)
             d_scores = (soft * (d_probs - delta) * scale).astype(bf16)
-            dv_acc[:seen, :] += jnp.dot(soft.astype(bf16), da, preferred_element_type=f32)
+            dv_acc[:seen, :] += jnp.dot(probs, da, preferred_element_type=f32)
             dk_acc[:seen, :] += jnp.dot(d_scores, q, preferred_element_type=f32)
             dq_t = rotate_back(jnp.dot(k_t[:, :seen], d_scores, preferred_element_type=f32), rows)
             dqkv_t[h, :, rows] = dq_t.astype(bf16)
@@ -567,13 +618,10 @@
     out.relay_ring(0)
     out.relay_ring(1)
 
-    for copy in parcel_copies:
-        copy.wait_send()
-    for step in hidden_steps[20:]:
+    for step in hidden_steps.values():
         step()
     for copy in inv_copies:
         copy.wait_recv()
-    load_kept.wait()
     for copy in weight_copies:
         copy.wait()
 
@@ -581,7 +629,7 @@
         columns = pl.ds(pl.multiple_of(n * TILE, TILE), TILE)
         return pltpu.make_async_copy(hidden_full.at[:, :, columns], tiles.at[:, :, pl.ds(pl.multiple_of(slot * TILE, TILE), TILE)], tile_sem.at[slot])
 
-    order = (0, 3, 1, 2)
+    order = (0, 1, 3, 2)
     tile_copy(4 * order[0], 0).start()
     for g, p in enumerate(order):
         following = order[g + 1] if g < 3 else None
@@ -620,6 +668,10 @@
             tree.begin_x(0, p)
         qkv.core_copy(2 * p).start()
         qkv.core_copy(2 * p + 1).start()
+        if g == 1:
+            out.send_half()
+        if g == 2:
+            qkv.begin_ring(0)
 
     gain_row = jnp.sum(gain_sum[...], axis=0, keepdims=True)
     for i in range(32):
@@ -629,21 +681,10 @@
 
     tree.relay(1, 0)
     tree.relay(0, 0)
-    qkv.begin_ring(0)
     qkv.begin_ring(1)
     tree.relay(1, 1)
     tree.relay(0, 1)
-    tree.z_done(2, 3)
-    tree.z_done(3, 3)
-    tree.begin_x(0, 3)
     qkv.relay_ring(0)
-    tree.root_other(0)
-    tree.relay(1, 2)
-    tree.relay(0, 2)
-    qkv.relay_ring(1)
-    tree.z_done(1, 3)
-    tree.root_other(1)
-    out.send_half()
 
     for copy in gain_copies:
         copy.wait_recv()
@@ -654,10 +695,19 @@
     gain_dp[d] = gain_total
     dp_copies = push_all(dp_peers, gain_block.at[1], gain_dp.at[d], gain_d_send, gain_d_recv)
 
+    tree.z_done(2, 3)
+    tree.z_done(3, 3)
+    tree.begin_x(0, 3)
+    qkv.relay_ring(1)
+    tree.root_other(0)
+    tree.relay(1, 2)
+    tree.relay(0, 2)
+    tree.z_done(1, 3)
+    tree.root_other(1)
     tree.relay(0, 3)
+    qkv.send_half()
     tree.z_done(0, 3)
     tree.root_other(2)
-    qkv.send_half()
     for b, value in enumerate(out.result()):
         gout_ref[b * 256:(b + 1) * 256, :] = value
 
@@ -697,6 +747,19 @@
         copy.wait_send()
 
 
+def hand_over(*refs):
+    sources, results, held, sems = refs[:6], refs[6:12], refs[12:18], refs[18]
+    loads = [pltpu.make_async_copy(sources[i], held[i], sems.at[0, i]) for i in range(6)]
+    stores = [pltpu.make_async_copy(held[i], results[i], sems.at[1, i]) for i in range(6)]
+    for copy in loads:
+        copy.start()
+    for before, after in zip(loads, stores):
+        before.wait()
+        after.start()
+    for copy in stores:
+        copy.wait()
+
+
 def per_device(
     hidden_in, teacher, row_source, segments, branch, queries, key_rot, value_rows, attended, norm_gain,
     w_query, w_key, w_value, w_out,
@@ -705,17 +768,15 @@
     vmem = pl.BlockSpec(memory_space=pltpu.VMEM)
     dma = pltpu.SemaphoreType.DMA
     scratch = pltpu.VMEM
-    frequency = (theta_base ** (-2.0 * np.arange(HD // 2, dtype=np.float64) / HD)).astype(np.float32)
-    frequency = np.broadcast_to(frequency[:, None], (HD // 2, 128))
     stage_sems = [dma((8,)), dma((8,)), dma((2, 6)), dma((2, 6)), dma((1,)), dma((1,))]
     shape = jax.ShapeDtypeStruct
-    d_hidden, grad_query, grad_key, grad_value, grad_out, grad_gain, _ = pl.pallas_call(
+    *results, _ = pl.pallas_call(
         kernel,
         out_shape=(
             shape((ROWS, D), f32), shape((256, 512), f32), shape((256, 128), f32), shape((256, 128), f32),
             shape((512, 256), f32), shape((32, 128), f32), shape((N_TENSOR, ROWS, D), bf16),
         ),
-        in_specs=[vmem] * 4 + [any_space] * 11,
+        in_specs=[vmem] * 3 + [any_space] * 11,
         out_specs=(vmem,) * 6 + (any_space,),
         scratch_shapes=[
             scratch((8, ROWS, D), bf16), scratch((8, ROWS, D), bf16), scratch((28, ROWS, STRIPE), bf16),
@@ -739,9 +800,17 @@
         ),
         cost_estimate=pl.CostEstimate(flops=27 * 10**9, bytes_accessed=60 * 2**20, transcendentals=4 * 2**20),
     )(
-        row_source[None, :], segments, frequency, norm_gain[None, :], teacher, branch, hidden_in, queries, key_rot, value_rows,
+        row_source[None, :], segments, norm_gain[None, :], teacher, branch, hidden_in, queries, key_rot, value_rows,
         attended, w_query, w_key, w_value, w_out,
     )
+    d_hidden, grad_query, grad_key, grad_value, grad_out, grad_gain = pl.pallas_call(
+        hand_over,
+        out_shape=[shape(value.shape, value.dtype) for value in results],
+        in_specs=[any_space] * 6,
+        out_specs=[any_space] * 6,
+        scratch_shapes=[scratch(value.shape, value.dtype) for value in results] + [dma((2, 6))],
+        compiler_params=pltpu.CompilerParams(vmem_limit_bytes=16 * 2**20),
+    )(*results)
     return (grad_query, grad_key, grad_value, grad_out, grad_gain.reshape(D), d_hidden)
 
 

time: 263 us -> 239 us (0.909)
  Pallas kernels: 249 us -> 232 us
  local copies, waits for them, and re-layouts: 12.7 us -> 6.19 us
    pallas_call x1, Pallas kernels: 249 us -> 229 us  [per_device(): pl.pallas_call(kernel, out_shape=(shape((ROWS, D), f32), shape((256, 512)...]
    unnamed x6 -> x12, local copies, waits for them, and re-layouts: 11.3 us -> 6.19 us
where the time goes in v3:
time: 239 us
  Pallas kernels  232 us (97%)
  local copies, waits for them, and re-layouts  6.19 us (3%)
    pallas_call x1, Pallas kernels, per_device(): pl.pallas_call(kernel, out_shape=(shape((ROWS, D), f32), shape((256, 512)...  229 us
    unnamed x12, local copies, waits for them, and re-layouts  6.19 us

profile of v3, /device:TPU:0, one launch (start us, length us, event | category | flops | bytes accessed | tf_op | source)
XLA Modules:
  0.0 238.6 jit_solution(3396258789483275429)
XLA Ops:
  0.6 229.2 %shard_map.181 = (f32[128,4096]{1,0:T(8,128)}, f32[256,512]{1,0:T(8,128)}, f32[256,128]{1,0:T(8,128)}, f32[256,128]{1,0:T(8,128)}, f32[512,256]{1,0:T(8,128)}, /...) custom-call(s32[1,128]{1,0:T(1,128)} %bitcast.5, s32[1,1024]{1,0:T(1,128)} %seg_ref.1, f32[1,4096]{1,0:T(1,128)} %bitcast.3, ...), custom_call_target="tpu_custom_call" | custom-call | flops 27000000512 | bytes 62914560 | tf_op jit(solution)/shard_map/pallas_call | solution.py:773
  229.8 0.0 copy-start
  229.8 1.6 copy-done
  231.4 0.0 copy-start.1
  231.4 1.0 copy-done.1
  232.4 0.0 copy-start.2
  232.4 1.0 copy-done.2
  233.5 0.0 copy-start.3
  233.5 0.9 copy-done.3
  234.4 0.0 copy-start.4
  234.4 0.9 copy-done.4
  235.3 0.0 copy-start.5
  235.3 0.7 copy-done.5
  236.0 2.4 %shard_map.182 = (f32[128,4096]{1,0:T(8,128)}, f32[256,512]{1,0:T(8,128)}, f32[256,128]{1,0:T(8,128)}, f32[256,128]{1,0:T(8,128)}, f32[512,256]{1,0:T(8,128)}, /*index=5*/f32[32,128]{1,0:T(8,128)}) custom-call(f32[128,4096]{1,0:T(8,128)S(1)} %copy-done, f32[256,512]{1,0:T(8,128)S(1)} %copy-done.1, f32[256,128]{1,0:T(8,128)S(1)} %copy-done.3, ...), custom_call_target="tpu_custom_call" | custom-call | tf_op jit(solution)/shard_map/pallas_call | solution.py:806
Async XLA Ops:
  229.8 1.6 copy-start
  231.4 1.0 copy-start.1
  232.4 1.0 copy-start.2
  233.5 0.9 copy-start.3
  234.4 0.9 copy-start.4
  235.3 0.7 copy-start.5

commit v4 on v3

--- a/solution.py
+++ b/solution.py
@@ -681,10 +681,10 @@
 
     tree.relay(1, 0)
     tree.relay(0, 0)
+    tree.z_done(2, 3)
     qkv.begin_ring(1)
-    tree.relay(1, 1)
-    tree.relay(0, 1)
     qkv.relay_ring(0)
+    tree.z_done(1, 3)
 
     for copy in gain_copies:
         copy.wait_recv()
@@ -695,18 +695,18 @@
     gain_dp[d] = gain_total
     dp_copies = push_all(dp_peers, gain_block.at[1], gain_dp.at[d], gain_d_send, gain_d_recv)
 
-    tree.z_done(2, 3)
+    tree.relay(1, 1)
+    tree.relay(0, 1)
     tree.z_done(3, 3)
     tree.begin_x(0, 3)
     qkv.relay_ring(1)
+    tree.z_done(0, 3)
     tree.root_other(0)
+    qkv.send_half()
     tree.relay(1, 2)
     tree.relay(0, 2)
-    tree.z_done(1, 3)
     tree.root_other(1)
     tree.relay(0, 3)
-    qkv.send_half()
-    tree.z_done(0, 3)
     tree.root_other(2)
     for b, value in enumerate(out.result()):
         gout_ref[b * 256:(b + 1) * 256, :] = value
@@ -809,7 +809,7 @@
         in_specs=[any_space] * 6,
         out_specs=[any_space] * 6,
         scratch_shapes=[scratch(value.shape, value.dtype) for value in results] + [dma((2, 6))],
-        compiler_params=pltpu.CompilerParams(vmem_limit_bytes=16 * 2**20),
+        compiler_params=pltpu.CompilerParams(vmem_limit_bytes=60 * 2**20),
     )(*results)
     return (grad_query, grad_key, grad_value, grad_out, grad_gain.reshape(D), d_hidden)
 

time: 239 us -> 234 us (0.979)
  local copies, waits for them, and re-layouts: 6.19 us -> 0 us
    unnamed x12 -> x0, local copies, waits for them, and re-layouts: 6.19 us -> none
where the time goes in v4:
time: 234 us; the launch traced here: 233 us
  Pallas kernels  232 us (99%)
    pallas_call x1, Pallas kernels, per_device(): pl.pallas_call(kernel, out_shape=(shape((ROWS, D), f32), shape((256, 512)...  229 us

profile of v4, /device:TPU:0, one launch (start us, length us, event | category | flops | bytes accessed | tf_op | source)
XLA Modules:
  0.0 233.2 jit_solution(12722200506399912662)
XLA Ops:
  0.6 228.9 %shard_map.181 = (f32[128,4096]{1,0:T(8,128)}, f32[256,512]{1,0:T(8,128)}, f32[256,128]{1,0:T(8,128)}, f32[256,128]{1,0:T(8,128)}, f32[512,256]{1,0:T(8,128)}, /...) custom-call(s32[1,128]{1,0:T(1,128)} %bitcast.5, s32[1,1024]{1,0:T(1,128)} %seg_ref.1, f32[1,4096]{1,0:T(1,128)} %bitcast.3, ...), custom_call_target="tpu_custom_call" | custom-call | flops 27000000512 | bytes 62914560 | tf_op jit(solution)/shard_map/pallas_call | solution.py:773
  229.5 3.4 %shard_map.182 = (f32[128,4096]{1,0:T(8,128)}, f32[256,512]{1,0:T(8,128)}, f32[256,128]{1,0:T(8,128)}, f32[256,128]{1,0:T(8,128)}, f32[512,256]{1,0:T(8,128)}, /*index=5*/f32[32,128]{1,0:T(8,128)}) custom-call(f32[128,4096]{1,0:T(8,128)} %get-tuple-element.18.refs_0_, f32[256,512]{1,0:T(8,128)} %get-tuple-element.19.refs_1_, ...), custom_call_target="tpu_custom_call" | custom-call | tf_op jit(solution)/shard_map/pallas_call | solution.py:806

commit v5 on v4

--- a/solution.py
+++ b/solution.py
@@ -519,11 +519,11 @@
     take(slope_steps, ("left", 0), ("right", 1))
     take(hidden_steps, ("partner", 2))
     take(slope_steps, ("far_left", 0), ("far_right", 1))
+    take(slope_steps, ("across", 2), ("across", 3))
     forward(3)
 
-    for p in (2, 3, 0, 1):
-        take(slope_steps, ("across", p))
-    take(slope_steps, ("left", 1), ("right", 0))
+    take(slope_steps, ("across", 0), ("across", 1), ("left", 1), ("right", 0))
+    take(hidden_steps, ("far_left", 2))
     for copy in load_w_out:
         copy.wait()
 
@@ -557,7 +557,6 @@
 
     attended_slope(z)
     lax.fori_loop(0, 16, out_gradient(z, True), 0)
-    take(hidden_steps, ("far_left", 2))
     for step in slope_steps.values():
         step()
     attended_slope(1 - z)
@@ -718,6 +717,12 @@
         gain_total = gain_total + gain_dp[k]
     ggain_ref[...] = gain_total
 
+    top, bottom = qkv.result()
+    gq_ref[:, :384] = top.T
+    gq_ref[:, 384:] = bottom[:128].T
+    gk_ref[...] = bottom[128:256].T
+    gv_ref[...] = bottom[256:].T
+
     for copy in loads[-4:]:
         copy.wait()
     inv = inv_own[:, 0:1]
@@ -733,11 +738,6 @@
         columns = slice(p * STRIPE, (p + 1) * STRIPE)
         unit = kept_hidden[p].astype(f32) * inv
         dh_ref[:, columns] = inv * (dh_ref[:, columns] - unit * mean)
-    top, bottom = qkv.result()
-    gq_ref[:, :384] = top.T
-    gq_ref[:, 384:] = bottom[:128].T
-    gk_ref[...] = bottom[128:256].T
-    gv_ref[...] = bottom[256:].T
 
     hidden_tree.finish()
     tree.finish()

time: 234 us -> 233 us (level)
  no operation moved by 1% of the time
where the time goes in v5:
time: 233 us
  Pallas kernels  232 us (100%)
    pallas_call x1, Pallas kernels, per_device(): pl.pallas_call(kernel, out_shape=(shape((ROWS, D), f32), shape((256, 512)...  228 us

profile of v5, /device:TPU:0, one launch (start us, length us, event | category | flops | bytes accessed | tf_op | source)
XLA Modules:
  0.0 232.7 jit_solution(13342277317755178285)
XLA Ops:
  0.6 228.4 %shard_map.181 = (f32[128,4096]{1,0:T(8,128)}, f32[256,512]{1,0:T(8,128)}, f32[256,128]{1,0:T(8,128)}, f32[256,128]{1,0:T(8,128)}, f32[512,256]{1,0:T(8,128)}, /...) custom-call(s32[1,128]{1,0:T(1,128)} %bitcast.5, s32[1,1024]{1,0:T(1,128)} %seg_ref.1, f32[1,4096]{1,0:T(1,128)} %bitcast.3, ...), custom_call_target="tpu_custom_call" | custom-call | flops 27000000512 | bytes 62914560 | tf_op jit(solution)/shard_map/pallas_call | solution.py:773
  229.0 3.4 %shard_map.182 = (f32[128,4096]{1,0:T(8,128)}, f32[256,512]{1,0:T(8,128)}, f32[256,128]{1,0:T(8,128)}, f32[256,128]{1,0:T(8,128)}, f32[512,256]{1,0:T(8,128)}, /*index=5*/f32[32,128]{1,0:T(8,128)}) custom-call(f32[128,4096]{1,0:T(8,128)} %get-tuple-element.18.refs_0_, f32[256,512]{1,0:T(8,128)} %get-tuple-element.19.refs_1_, ...), custom_call_target="tpu_custom_call" | custom-call | tf_op jit(solution)/shard_map/pallas_call | solution.py:806
